TPU v7x, 32 devices: a whole 2x2x4 slice. The times are simulated.
32 devices in a mesh: narrow: 8 (over z, core), wide: 4 (over y, x).
Axes of the slice: x: 2, y: 2, z: 4, core: 2. Of those that a mesh axis runs over, the one named last changes fastest.
Arguments:
- frames_in: bfloat16 [16, 1536, 768], P('narrow', 'wide'), may hold values from -6 to 6
- lengths: int32 [16], P('narrow'), may hold values from 102 to 1536, as said below
- kernel: bfloat16 [128, 16, 48, 48], replicated, may hold values from -0.15625 to 0.15625
- conv_bias: bfloat16 [768], replicated, may hold values from -3 to 3
- w_query: bfloat16 [768, 768], replicated, may hold values from -0.21875 to 0.21875
- b_query: bfloat16 [768], replicated, may hold values from -3 to 3
- w_key: bfloat16 [768, 768], replicated, may hold values from -0.21875 to 0.21875
- w_value: bfloat16 [768, 768], replicated, may hold values from -0.21875 to 0.21875
- b_value: bfloat16 [768], replicated, may hold values from -3 to 3
- w_out: bfloat16 [768, 768], replicated, may hold values from -1.25 to 1.25
- b_out: bfloat16 [768], replicated, may hold values from -3 to 3
- gain_one: bfloat16 [768], replicated, may hold values from 0.25 to 1.75
- shift_one: bfloat16 [768], replicated, may hold values from -3 to 3
- w_up: bfloat16 [768, 3072], replicated, may hold values from -0.21875 to 0.21875
- b_up: bfloat16 [3072], replicated, may hold values from -3 to 3
- w_down: bfloat16 [3072, 768], replicated, may hold values from -0.109375 to 0.109375
- b_down: bfloat16 [768], replicated, may hold values from -3 to 3
- gain_two: bfloat16 [768], replicated, may hold values from 0.25 to 1.75
- shift_two: bfloat16 [768], replicated, may hold values from -3 to 3
- out_grad: bfloat16 [16, 1536, 768], P('narrow', 'wide'), may hold values from -6 to 6
Outputs:
- layer_out: bfloat16 [16, 1536, 768], P('narrow', 'wide')
- frames_grad: bfloat16 [16, 1536, 768], P('narrow', 'wide')
- grad_kernel: float32 [128, 16, 48, 48], P('wide')
- grad_conv_bias: float32 [768], P('wide')
- grad_w_query: float32 [768, 768], P('wide')
- grad_b_query: float32 [768], P('wide')
- grad_w_key: float32 [768, 768], P('wide')
- grad_w_value: float32 [768, 768], P('wide')
- grad_b_value: float32 [768], P('wide')
- grad_w_out: float32 [768, 768], P('wide')
- grad_b_out: float32 [768], P('wide')
- grad_gain_one: float32 [768], P('wide')
- grad_shift_one: float32 [768], P('wide')
- grad_w_up: float32 [768, 3072], P('wide')
- grad_b_up: float32 [3072], P('wide')
- grad_w_down: float32 [3072, 768], P('wide')
- grad_b_down: float32 [768], P('wide')
- grad_gain_two: float32 [768], P('wide')
- grad_shift_two: float32 [768], P('wide')
Inputs may be any that keep to these rules, and one draw needn't show every extreme that they name: `lengths`: among the 2 clips of each index of narrow, one has exactly 1536 frames and another exactly 102.
All inputs are finite; a program needn't handle non-finite values.
Results may differ from a plain program's by a relative error of at most 0.025.
The roundings to bfloat16 on the way count: a program that leaves them out, or rounds other values in their place, can miss the bound.
Values may be sent and summed in bfloat16 or wider, within the bound.
A program may use at most 320 MiB of HBM per device.

v0:
```python
import functools

import jax
import jax.numpy as jnp
from jax import lax
from jax.experimental import pallas as pl
from jax.experimental.pallas import tpu as pltpu
from jax.sharding import PartitionSpec as P

HEADS = 12
GROUP_CH = 48
SHORT = 102
HALF = 64
UNIQUE = SHORT + HALF
FR = 384
SLOTS = 1536
SROWS = 192
TROWS = 1792
SBASE = 1600
CH = 192
eps_norm = 1e-05
neg_large = -1e30
bf16 = jnp.bfloat16
f32 = jnp.float32
QF = 1536
QB = 768
KB = 512
CB = 1792
VLIM = 60 * 1024 * 1024


def mm(a, b):
    return jnp.dot(a, b, preferred_element_type=f32)


def mm_nt(a, b):
    return lax.dot_general(a, b, (((1,), (1,)), ((), ())), preferred_element_type=f32)


def iota2(shape):
    return lax.broadcasted_iota(jnp.int32, shape, 0), lax.broadcasted_iota(jnp.int32, shape, 1)


def place(shape, rows_from, rows_to, cols_from):
    r, c = iota2(shape)
    hit = (c - cols_from == r - rows_from) & (r >= rows_from) & (r < rows_to)
    return hit.astype(f32).astype(bf16)


def spread(shape, lane0, start):
    r, c = iota2(shape)
    slot, inner = c >> 6, c & 63
    hit = (r == lane0 + start + slot * GROUP_CH + inner) & (inner < GROUP_CH)
    return hit.astype(f32).astype(bf16)


def gather_slots(shape, col0):
    r, c = iota2(shape)
    slot, inner = r >> 6, r & 63
    hit = (c == col0 + slot * GROUP_CH + inner) & (inner < GROUP_CH)
    return hit.astype(f32).astype(bf16)


def full(shape):
    return pl.BlockSpec(shape, lambda *_: (0,) * len(shape))


def smem():
    return pl.BlockSpec(memory_space=pltpu.SMEM)


def vmem():
    return pl.BlockSpec(memory_space=pltpu.VMEM)


def params(**kw):
    return pltpu.CompilerParams(vmem_limit_bytes=VLIM, **kw)


def cost(us):
    return pl.CostEstimate(flops=int(us * 1e9), bytes_accessed=int(us * 3.4e6), transcendentals=0)


def put(keeping, keep, send, rel, row0, data, lane0=0):
    rows, lanes = data.shape

    @pl.when(keeping)
    def _():
        keep[rel, row0 : row0 + rows, lane0 : lane0 + lanes] = data

    @pl.when(jnp.logical_not(keeping))
    def _():
        send[rel, row0 : row0 + rows, lane0 : lane0 + lanes] = data


def xor2(a, b):
    return (a + b) % 2 + 2 * ((a // 2 + b // 2) % 2)


def gelu_parts(v):
    cdf = 0.5 * (1.0 + lax.erf(v * (2.0 ** -0.5)))
    return cdf


def density(v):
    return jnp.exp(-0.5 * v * v) * 0.3989422804014327


def pack_frames_kernel(s_ref, x_ref, *outs):
    me, li = s_ref[0], s_ref[1]
    long, short = x_ref[li], x_ref[1 - li]
    slot = me * FR + lax.broadcasted_iota(jnp.int32, (128, 768), 0)
    short = jnp.where(slot < SHORT, short[:128].astype(f32), 0.0).astype(bf16)
    top = long[:256]
    low = jnp.concatenate([long[256:], short], axis=0)
    for d in range(4):
        first = 192 * d - (64 if d % 2 else 0)
        skip = 64 if d % 2 else 0
        chunk = mm(top[:, first : first + 256], place((256, 384), skip, skip + 192, 0)) + mm(
            low[:, first : first + 256], place((256, 384), skip, skip + 192, 192)
        )
        chunk = chunk.astype(bf16)
        for r in range(4):

            @pl.when((me ^ d) == r)
            def _():
                outs[r][...] = chunk


def pack_frames(scal, frames_in):
    return pl.pallas_call(
        pack_frames_kernel,
        out_shape=[jax.ShapeDtypeStruct((256, 384), bf16)] * 4,
        in_specs=[smem(), vmem()],
        out_specs=[vmem()] * 4,
        compiler_params=params(),
        cost_estimate=cost(3),
        name="pack_frames",
    )(scal, frames_in)


def prep_group(w_ref, wt_ref, wd_ref, z_ref, taps):
    left, right = place((48, 128), 0, 48, 0), place((48, 128), 0, 48, 64)
    wt_ref[...] = jnp.zeros_like(wt_ref)
    for i in range(48):
        taps[pl.ds(i, 128, stride=48), 0:48] = w_ref[i].astype(f32).T

    def rows(k, n):
        return taps[48 * k : 48 * (k + n), 0:48].astype(bf16)

    for k2 in range(8):
        pairs = rows(16 * k2, 16).reshape(8, 2, 48, 48)
        tile = mm(pairs[:, 0].reshape(384, 48), left) + mm(pairs[:, 1].reshape(384, 48), right)
        tile = tile.astype(bf16)
        for p in range(8):
            wt_ref[64 * k2 : 64 * k2 + 48, 128 * p : 128 * p + 128] = tile[48 * p : 48 * p + 48]
    for q in range(4):
        tile = mm(rows(112 - 32 * q, 16), left) + mm(rows(96 - 32 * q, 16), right)
        for b in range(16):
            z_ref[64 * b : 64 * b + 48, :] = tile[48 * (15 - b) : 48 * (15 - b) + 48]
        wd_ref[128 * q : 128 * q + 128, :] = z_ref[...].T.astype(bf16)


def pair_slots(t_ref, rows):
    wide = jnp.concatenate([t_ref[0:rows, :], t_ref[16 : rows + 16, :]], axis=1)
    r, c = iota2((256, 128))
    out = []
    for j in range(2):
        hit = ((r < 128) & (c == r - 64 * j) & (c < 64)) | ((r >= 128) & (c - 64 == r - 128 - 64 * j) & (c >= 64))
        out.append(mm(wide, hit.astype(f32).astype(bf16)).astype(bf16))
    return out


def conv_block(p_refs, w_ref, y_ref, s_ref, shift, n0=0, rows=CB):
    lane = lax.broadcasted_iota(jnp.int32, (rows, 128), 1)
    parts = []
    for j in range(2):
        lhs = jnp.concatenate([p_refs[j][n0 + 32 * q : n0 + 32 * q + rows + 16, :] for q in range(4)], axis=1)
        y_ref[0 : rows + 16] = mm(lhs, w_ref[j])
        total = y_ref[shift : shift + rows + 1, 0:128]
        for p in range(1, 8):
            total += y_ref[shift + 2 * p : shift + 2 * p + rows + 1, 128 * p : 128 * p + 128]
        s_ref[0 : rows + 1, :] = total
        here, after = s_ref[0:rows, :], s_ref[1 : rows + 1, :]
        if j == 0:
            parts.append(here + pltpu.roll(after, 64, 1))
        else:
            parts.append(pltpu.roll(here, 64, 1) + after)
    return jnp.where(lane < 64, parts[0], parts[1])


def front_sync_kernel(
    p0, p1, p2, p3, k_hbm, vec, wq, wk, wv,
    wd, pre_ref, xp, h0, h1, h2, h3, qkv, ot, lse_ref, rows_ref, w_own, m0, m1, m2, m3,
    kg, load_s, wt, taps, zt, rf, slots, y_ref, t_ref, first, wz, vt, o1, o2, o3, frame_s, frame_r, gat_s, gat_r, mix_s, mix_r,
):
    n, me = lax.axis_index("narrow"), lax.axis_index("wide")
    barrier = pltpu.get_barrier_semaphore()

    def device(r):
        return (n, xor2(me, r))

    for r in range(1, 4):
        pl.semaphore_signal(barrier, inc=1, device_id=device(r), device_id_type=pl.DeviceIdType.MESH)
    load = pltpu.make_async_copy(k_hbm.at[pl.ds(4 * me, 4)], kg, load_s)
    load.start()
    pl.semaphore_wait(barrier, 3)

    def copy(r, src, dst, send, recv):
        return pltpu.make_async_remote_copy(
            src_ref=src, dst_ref=dst, send_sem=send, recv_sem=recv, device_id=device(r),
            device_id_type=pl.DeviceIdType.MESH,
        )

    frames = [copy(r, (p1, p2, p3)[r - 1], rf.at[r - 1], frame_s.at[r - 1], frame_r.at[r - 1]) for r in (3, 1, 2)]
    for c in frames:
        c.start()

    zt[...] = jnp.zeros_like(zt)
    load.wait()

    def prep(g, carry):
        prep_group(kg.at[g], wt.at[g], wd.at[g], zt, taps)
        return carry

    lax.fori_loop(0, 4, prep, 0)
    r_i, c_i = iota2((768, 256))
    pick = ((r_i == 192 * me + c_i) & (c_i < 192)).astype(f32).astype(bf16)
    for k, w in enumerate((wq, wk, wv)):
        w_own[:, 256 * k : 256 * k + 256] = mm(w[...], pick).astype(bf16)
    own_vec = mm(vec[...], pick)
    bias_qkv = jnp.concatenate([own_vec[1:2], jnp.zeros((1, 256), f32), own_vec[2:3]], axis=1)
    bias = [mm(vec[...], spread((768, 128), 0, 192 * me + 96 * c))[0:1] for c in range(2)]
    wz[:, 0:64, :] = jnp.zeros((4, 64, 768), bf16)
    wz[:, 256:320, :] = jnp.zeros((4, 64, 768), bf16)
    for r in range(4):
        wz[r, 64:256, :] = w_own[pl.ds(pl.multiple_of(192 * xor2(me, r), 64), 192), :]

    for c in frames:
        c.wait()
    for c in range(2):
        xp[c, 0:64, :] = jnp.zeros((64, 128), bf16)
        xp[c, 1600:1664, :] = jnp.zeros((64, 128), bf16)
        xp[c, 1792:1936, :] = jnp.zeros((144, 128), bf16)
        top_map, low_map = spread((256, 128), 0, 96 * c), spread((256, 128), 64, 96 * c)
        short = jnp.zeros((128, 128), f32)
        for r in range(4):
            src = xor2(me, r)
            chunk = p0 if r == 0 else rf.at[r - 1]
            low = mm(chunk[:, 128:384], low_map)
            base = pl.multiple_of(64 + FR * src, 64)
            xp[c, pl.ds(base, 256), :] = mm(chunk[:, 0:256], top_map).astype(bf16)
            xp[c, pl.ds(pl.multiple_of(base + 256, 64), 128), :] = low[:128].astype(bf16)
            short += jnp.where(src == 0, low[128:], 0.0)
        xp[c, 1664:1792, :] = short.astype(bf16)
        a, b = pair_slots(xp.at[c], 1920)
        slots[2 * c] = a
        slots[2 * c + 1] = b

    left, right = gather_slots((256, 384), 0), gather_slots((256, 384), 192)

    def rows_of(lo, rows):
        return jnp.concatenate([first[0, lo : lo + rows, :], first[1, lo : lo + rows, :]], axis=1)

    held = (h0, h1, h2, h3)
    spans = [(0, 384), (384, 384), (768, 96)]

    def direct(i, r):
        at = pl.ds(*spans[i])
        return copy(r, h0.at[at], held[r].at[at], gat_s.at[4 * i + r - 1], gat_r.at[4 * i + r - 1])

    def relay(i, r):
        row, rows = spans[i]
        at = pl.ds(row, rows // 2) if r == 1 else pl.ds(row + rows // 2, rows // 2)
        sem = 4 * i + 1 + r
        return copy(3 - r, held[r].at[at], h3.at[at], gat_s.at[sem], gat_r.at[sem])

    def conv(block):
        n0 = 896 * block
        for c in range(2):
            pre = conv_block((slots.at[2 * c], slots.at[2 * c + 1]), wt.at[2 * c : 2 * c + 2], y_ref, t_ref, 0, n0, 896)
            pre = pre + bias[c]
            pre_ref[c, n0 : n0 + 896, :] = pre
            center = xp[c, 64 + n0 : 64 + n0 + 896, :].astype(f32)
            first[c, n0 : n0 + 896, :] = (center + pre * gelu_parts(pre)).astype(bf16)

    def pack(row, lo, rows):
        h0[row : row + rows, :] = (mm(rows_of(lo, rows), left) + mm(rows_of(lo + rows, rows), right)).astype(bf16)

    conv(0)
    pack(0, 0, 384)
    for r in (1, 2):
        direct(0, r).start()
    conv(1)
    pack(384, 768, 384)
    pack(768, SBASE, 96)
    for i in (1, 2):
        for r in (1, 2):
            direct(i, r).start()
    for i in range(3):
        for r in (1, 2):
            direct(i, r).wait()
            relay(i, r).start()
    for i in range(3):
        for r in (1, 2):
            relay(i, r).wait()

    def project(row, rows, half):
        row0 = 64 * (1 - half)
        total = bias_qkv + jnp.zeros((rows, 768), f32)
        for r in range(4):
            total += mm(held[r][row : row + rows, 128 * half : 128 * half + 256], wz[r, row0 : row0 + 256, :])
        return total.astype(bf16)

    for half in range(2):
        qkv[384 * half : 384 * half + 384, :] = project(0, 384, half)
        qkv[768 + 384 * half : 1152 + 384 * half, :] = project(384, 384, half)
        qkv[SLOTS + 96 * half : SLOTS + 96 * half + 96, :] = project(768, 96, half)
    qkv[SLOTS + SROWS : TROWS, :] = jnp.zeros((TROWS - SLOTS - SROWS, 768), bf16)
    vt[...] = qkv[:, 512:704].astype(f32).T.astype(bf16)

    outs = (m0, o1, o2, o3)
    lse_ref[...] = jnp.zeros_like(lse_ref)
    sent = []
    for h in range(3):
        cols = slice(64 * h, 64 * h + 64)

        def attend(q0, queries, key0, keys, masked):
            query = (qkv[q0 : q0 + queries, 0:256][:, cols].astype(f32) * 0.125).astype(bf16)
            key = qkv[key0 : key0 + keys, 256:512][:, cols]
            scores = mm_nt(key, query)
            if masked:
                slot = lax.broadcasted_iota(jnp.int32, scores.shape, 0)
                scores = jnp.where(slot < SHORT, scores, neg_large)
            top = jnp.max(scores, axis=0, keepdims=True)
            weights = jnp.exp(scores - top)
            total = jnp.sum(weights, axis=0, keepdims=True)
            out = mm(vt[cols, key0 : key0 + keys], weights.astype(bf16))
            ot[cols, q0 : q0 + queries] = out / total
            lse_ref[h : h + 1, q0 : q0 + queries] = top + jnp.log(total)

        for q0 in range(0, SLOTS, QF):
            attend(q0, QF, 0, SLOTS, False)
        attend(SLOTS, 256, SLOTS, 128, True)
        for r in (3, 1, 2, 0):
            src = pl.multiple_of(FR * xor2(me, r), 128)
            outs[r][cols, 0:FR] = ot[cols, pl.ds(src, FR)].astype(bf16)
            outs[r][cols, FR:640] = ot[cols, SLOTS:TROWS].astype(bf16)
            if r:
                at = pl.ds(64 * h, 64)
                sem = 3 * h + r - 1
                c = copy(r, outs[r].at[at], (m1, m2, m3)[r - 1].at[at], mix_s.at[sem], mix_r.at[sem])
                c.start()
                sent.append(c)

    start = pl.multiple_of(FR * (me // 2), 128)
    lane0 = pl.multiple_of(128 * (me % 2), 128)
    r_i, c_i = iota2((256, 768))
    own = jnp.zeros((FR, 768), f32)
    extra0 = jnp.zeros((96, 768), f32)
    extra1 = jnp.zeros((96, 768), f32)
    for r in range(4):
        base = 192 * xor2(me, r)
        inside = (c_i >= base) & (c_i < base + 192)
        sel0 = ((c_i - base == r_i) & inside).astype(f32).astype(bf16)
        sel1 = ((c_i - base == r_i - 64) & inside).astype(f32).astype(bf16)
        own += mm(held[r][pl.ds(start, FR), pl.ds(lane0, 256)], jnp.where(me % 2 == 0, sel0, sel1))
        extra0 += mm(held[r][768:864, 0:256], sel0)
        extra1 += mm(held[r][768:864, 128:384], sel1)
    rows_ref[0:FR, :] = own.astype(bf16)
    rows_ref[FR : FR + 96, :] = extra0.astype(bf16)
    rows_ref[FR + 96 : FR + 192, :] = extra1.astype(bf16)
    for c in sent:
        c.wait()


def front_sync(chunks, kernel, vec, wq, wk, wv):
    sds = jax.ShapeDtypeStruct
    sem = pltpu.SemaphoreType.DMA
    room = lambda *shape: pltpu.VMEM(shape, bf16)
    return pl.pallas_call(
        front_sync_kernel,
        in_specs=[vmem()] * 4 + [pl.BlockSpec(memory_space=pl.ANY)] + [vmem()] * 4,
        out_specs=[vmem()] * 16,
        out_shape=[sds((4, 512, 1024), bf16), sds((2, TROWS, 128), f32), sds((2, 1936, 128), bf16)]
        + [sds((864, 384), bf16)] * 4
        + [sds((TROWS, 768), bf16), sds((CH, TROWS), f32), sds((8, TROWS), f32), sds((576, 768), bf16)]
        + [sds((768, 768), bf16)]
        + [sds((CH, 640), bf16)] * 4,
        scratch_shapes=[
            room(4, 48, 48, 128),
            sem,
            room(4, 512, 1024),
            pltpu.VMEM((48 * 128, 128), f32),
            pltpu.VMEM((1024, 128), f32),
            room(3, 256, 384),
            room(4, 1920, 128),
            pltpu.VMEM((912, 1024), f32),
            pltpu.VMEM((904, 128), f32),
            room(2, TROWS, 128),
            room(4, 320, 768),
            room(CH, TROWS),
        ]
        + [room(CH, 640)] * 3
        + [sem((3,)), sem((3,)), sem((12,)), sem((12,)), sem((9,)), sem((9,))],
        compiler_params=params(collective_id=3, has_side_effects=True),
        cost_estimate=cost(65),
        name="front_sync",
    )(*chunks, jnp.transpose(kernel, (1, 2, 3, 0)), vec, wq, wk, wv)


def attn_sync_kernel(
    qkv_ref, ot_ref, lse_ref, d0, d1, d2, d3, gst, w_ref, h0, h1, h2, h3,
    nl, gd, ul_hbm, gu_hbm, m0, m1, m2, m3, gac, sums,
    a1_out, a2_out, b_out, g_out, qsums,
    ring, load_s, dot_, do_, kt, delta, dqt, dk, dv, dqkv, keep1, send1, got1, keep2, send2, got2,
    bkeep, bsend, bgot, ra, rd, g0, g1, g2, g3, rg, core_s, core_r, wide_s, wide_r,
):
    n, me = lax.axis_index("narrow"), lax.axis_index("wide")
    core = n % 2
    other = n + 1 - 2 * core
    MESH = pl.DeviceIdType.MESH

    barrier = pltpu.get_barrier_semaphore()
    peers = [(n, xor2(me, r)) for r in range(1, 4)] + [(other, me)]
    for peer in peers:
        pl.semaphore_signal(barrier, inc=1, device_id=peer, device_id_type=MESH)

    def load(i):
        if i < 4:
            j = 2 * (1 - core) + i if i < 2 else 2 * core + i - 2
            src = gu_hbm.at[:, pl.ds(pl.multiple_of(768 * j, 128), 768)]
        else:
            src = ul_hbm.at[:, 768 * (i - 4) : 768 * (i - 3)]
        return pltpu.make_async_copy(src, ring.at[i % 2], load_s.at[i])

    load(0).start()
    load(1).start()
    pl.semaphore_wait(barrier, 4)

    def to_wide(i, r, src, dst):
        return pltpu.make_async_remote_copy(
            src_ref=src, dst_ref=dst, send_sem=wide_s.at[i], recv_sem=wide_r.at[i],
            device_id=(n, xor2(me, r)), device_id_type=MESH,
        )

    def to_core(i, src, dst):
        return pltpu.make_async_remote_copy(
            src_ref=src, dst_ref=dst, send_sem=core_s.at[i], recv_sem=core_r.at[i],
            device_id=(other, me), device_id_type=MESH,
        )

    send_d = [to_wide(r - 1, r, (d1, d2, d3)[r - 1], rd.at[r - 1]) for r in (3, 1, 2)]
    for c in send_d:
        c.start()

    core1, core2, coreb = to_core(0, send1, got1), to_core(1, send2, got2), to_core(2, bsend, bgot)
    for i in range(4):
        load(i).wait()
        up = tn(nl[...], ring[i % 2]).astype(bf16)
        to = send1 if i < 2 else keep1
        row = 192 * (i % 2)
        for e in range(4):
            to[xor2(me, e), row : row + 192, :] = up[192 * e : 192 * e + 192]
        load(i + 2).start()
        if i == 1:
            core1.start()
    extra = jnp.concatenate([sums[...], jnp.zeros((48, 768), f32)], axis=0).astype(bf16)
    for j in range(4):
        load(4 + j).wait()
        down = tn(ring[j % 2], gd[...]).astype(bf16)
        rel = xor2(me, j)
        put(core == 0, keep2, send2, rel, 0, down[0:512])
        put(core == 1, keep2, send2, rel, 0, down[512:768])
        if j < 2:
            load(6 + j).start()
    for r, m in enumerate((m0, m1, m2, m3)):
        put(core == 1, keep2, send2, r, 256, mm(m[...], gac[...]).astype(bf16))
        put(core == 1, keep2, send2, r, 448, extra)
    core2.start()
    core1.wait()
    for r in range(4):
        keep1[r] = (keep1[r].astype(f32) + got1[r].astype(f32)).astype(bf16)
    send_a = [to_wide(2 + r, r, keep1.at[r], ra.at[r - 1]) for r in (3, 1, 2)]
    for c in send_d:
        c.wait()
    for c in send_a:
        c.start()

    short = d0[:, FR : FR + 256].astype(f32)
    dot_[:, pl.ds(pl.multiple_of(FR * me, 128), FR)] = d0[:, 0:FR]
    for r in range(1, 4):
        dot_[:, pl.ds(pl.multiple_of(FR * xor2(me, r), 128), FR)] = rd[r - 1, :, 0:FR]
        short += rd[r - 1, :, FR : FR + 256].astype(f32)
    dot_[:, SLOTS:TROWS] = short.astype(bf16)
    whole = dot_[...].astype(f32)
    do_[...] = whole.T.astype(bf16)
    prod = whole * ot_ref[...]
    for h in range(3):
        delta[h : h + 1, :] = jnp.sum(prod[64 * h : 64 * h + 64], axis=0, keepdims=True)
    kt[...] = qkv_ref[:, 256:448].astype(f32).T.astype(bf16)
    keep_k, keep_v = [], []
    for h in range(3):
        cols = slice(64 * h, 64 * h + 64)
        dk[...] = jnp.zeros_like(dk)
        dv[...] = jnp.zeros_like(dv)

        def step(q0, queries, key0, keys, masked):
            at_q = pl.ds(q0, queries)
            query = qkv_ref[at_q, 0:256][:, cols]
            scaled = (query.astype(f32) * 0.125).astype(bf16)
            grad = do_[at_q, :][:, cols]
            grad_t = dot_[cols, at_q]
            lse = lse_ref[h : h + 1, at_q]
            dl = delta[h : h + 1, at_q]
            grad_q = jnp.zeros((64, queries), f32)
            piece = min(keys, KB)
            for at in range(key0, key0 + keys, piece):
                key = qkv_ref[at : at + piece, 256:512][:, cols]
                val = qkv_ref[at : at + piece, 512:768][:, cols]
                probs = jnp.exp(mm_nt(key, scaled) - lse)
                if masked:
                    slot = lax.broadcasted_iota(jnp.int32, probs.shape, 0)
                    probs = jnp.where(slot < SHORT, probs, 0.0)
                grad_p = mm(val, grad_t)
                grad_s = (probs * (grad_p - dl)).astype(bf16)
                dv[at : at + piece, :] += mm(probs.astype(bf16), grad)
                dk[at : at + piece, :] += mm(grad_s, query)
                grad_q += mm(kt[cols, at : at + piece], grad_s)
            dqt[cols, at_q] = grad_q * 0.125

        for q0 in range(0, SLOTS, QB):
            step(q0, QB, 0, SLOTS, False)
        step(SLOTS, 256, SLOTS, 128, True)
        keep_k.append((dk[...] * 0.125).astype(bf16))
        keep_v.append(dv[...].astype(bf16))
    zeros = jnp.zeros((TROWS, 64), bf16)
    dqkv[:, 0:192] = dqt[...].T.astype(bf16)
    dqkv[:, 192:256] = zeros
    dqkv[:, 256:512] = jnp.concatenate(keep_k + [zeros], axis=1)
    dqkv[:, 512:768] = jnp.concatenate(keep_v + [zeros], axis=1)

    parts = (g0, g1, g2, g3)
    lanes = pl.multiple_of(FR * me, 128)
    near, far = slice(0, 896), slice(896, TROWS)

    def project(r):
        rows = pl.ds(pl.multiple_of(192 * xor2(me, r), 64), 192)
        part = mm_nt(w_ref[rows, :], dqkv[...])
        parts[r][...] = part.astype(bf16)
        own = gst[rows, 0:FR].astype(f32)
        parts[r][:, pl.ds(lanes, FR)] = (parts[r][:, pl.ds(lanes, FR)].astype(f32) + own).astype(bf16)
        parts[r][:, SLOTS:TROWS] = (part[:, SLOTS:TROWS] + gst[rows, FR : FR + 256].astype(f32)).astype(bf16)

    def hop(i, r, src, half):
        return to_wide(6 + i, r, src.at[:, half], rg.at[i])

    first = [hop(0, 1, g3, near), hop(1, 2, g3, far), hop(2, 1, g1, near), hop(3, 2, g2, far)]
    second = [hop(4, 2, g2, near), hop(5, 1, g1, far)]
    project(3)
    first[0].start()
    first[1].start()
    project(1)
    first[2].start()
    project(2)
    first[3].start()
    project(0)
    qsums[...] = jnp.sum(dqkv[...].astype(f32), axis=0, keepdims=True)

    def join(part, half, i):
        part[:, half] = (part[:, half].astype(f32) + rg[i].astype(f32)).astype(bf16)

    def chunk_grad(chunk, r):
        turned = chunk[...].astype(f32).T.astype(bf16)
        value = (
            mm(turned[0:192, 0:384], dqkv[0:384, :])
            + mm(turned[192:384, 0:384], dqkv[384:768, :])
            + mm(turned[0:192, 384:768], dqkv[768:1152, :])
            + mm(turned[192:384, 384:768], dqkv[1152:1536, :])
            + mm(turned[0:192, 768:864], dqkv[SLOTS : SLOTS + 96, :])
            + mm(turned[192:384, 768:864], dqkv[SLOTS + 96 : SLOTS + 192, :])
        ).astype(bf16)
        put(core == 0, bkeep, bsend, r, 0, value[0:96])
        put(core == 1, bkeep, bsend, r, 0, value[96:192])

    chunk_grad(h0, 0)
    chunk_grad(h1, 1)
    for c in send_a:
        c.wait()
    a1_out[...] = (keep1[0].astype(f32) + ra[0].astype(f32) + ra[1].astype(f32) + ra[2].astype(f32)).astype(bf16)
    first[0].wait()
    join(g2, near, 0)
    second[0].start()
    first[1].wait()
    join(g1, far, 1)
    second[1].start()
    chunk_grad(h2, 2)
    chunk_grad(h3, 3)
    coreb.start()
    core2.wait()
    for r in range(4):
        a2_out[r] = (keep2[r].astype(f32) + got2[r].astype(f32)).astype(bf16)
    first[2].wait()
    first[3].wait()
    coreb.wait()
    for r in range(4):
        b_out[r] = (bkeep[r].astype(f32) + bgot[r].astype(f32)).astype(bf16)
    second[0].wait()
    g_out[:, near] = g0[:, near].astype(f32) + rg[2].astype(f32) + rg[4].astype(f32)
    second[1].wait()
    g_out[:, far] = g0[:, far].astype(f32) + rg[3].astype(f32) + rg[5].astype(f32)


def attn_sync(qkv, ot, lse, dparts, gst, wqkv, first, nl, gd, ul, gu, mix, gac, sums):
    sds = jax.ShapeDtypeStruct
    hbm = pl.BlockSpec(memory_space=pl.ANY)
    sem = pltpu.SemaphoreType.DMA
    room = lambda *shape: pltpu.VMEM(shape, bf16)
    return pl.pallas_call(
        attn_sync_kernel,
        in_specs=[vmem()] * 15 + [hbm] * 2 + [vmem()] * 6,
        out_specs=[vmem()] * 5,
        out_shape=[
            sds((384, 768), bf16), sds((4, 512, 768), bf16), sds((4, 96, 768), bf16), sds((CH, TROWS), f32),
            sds((1, 768), f32),
        ],
        scratch_shapes=[
            room(2, 768, 768),
            sem((8,)),
            room(CH, TROWS),
            room(TROWS, CH),
            room(CH, TROWS),
            pltpu.VMEM((8, TROWS), f32),
            pltpu.VMEM((CH, TROWS), f32),
            pltpu.VMEM((TROWS, 64), f32),
            pltpu.VMEM((TROWS, 64), f32),
            room(TROWS, 768),
        ]
        + [room(4, 384, 768)] * 3
        + [room(4, 512, 768)] * 3
        + [room(4, 96, 768)] * 3
        + [room(3, 384, 768), room(3, CH, 640)]
        + [room(CH, TROWS)] * 4
        + [room(6, CH, 896), sem((3,)), sem((3,)), sem((12,)), sem((12,))],
        compiler_params=params(collective_id=2, has_side_effects=True),
        cost_estimate=cost(90),
        name="attn_sync",
    )(qkv, ot, lse, *dparts, gst, wqkv, *first, nl, gd, ul, gu, *mix, gac, sums)


def wgrad_pair(pair, me, gsum, pre_ref, x_ref, sums_ref, half, gf, g_ref, gp, p0, p1, bb, g2, xt):
    at = pl.ds(pl.multiple_of(96 * pair, 32), 96)
    total = gsum[at, :]
    pad = jnp.zeros((16, TROWS), f32)
    rows = jnp.concatenate([total[0:48], pad, total[48:96], pad], axis=0)
    gf[0:SLOTS, :] = rows[:, 0:SLOTS].T
    gf[SLOTS:SBASE, :] = jnp.zeros((SBASE - SLOTS, 128), f32)
    gf[SBASE:TROWS, :] = rows[:, SLOTS:TROWS].T[0 : TROWS - SBASE]
    g_ref[0:64, :] = jnp.zeros((64, 128), bf16)
    g_ref[1856:1936, :] = jnp.zeros((80, 128), bf16)
    gp[0:16, :] = jnp.zeros((16, 128), f32)
    pre = pre_ref[pair]
    slope = gelu_parts(pre) + pre * density(pre)
    wide = (gf[...] * slope).astype(bf16).astype(f32)
    bias_sum = jnp.sum(wide, axis=0, keepdims=True)
    row = lax.broadcasted_iota(jnp.int32, (TROWS, 128), 0)
    wide = jnp.where(row < SBASE + UNIQUE, wide, 0.0)
    gp[16 : 16 + TROWS, :] = wide
    g_ref[64 : 64 + TROWS, :] = wide.astype(bf16)
    extra = jnp.concatenate(
        [sums_ref[...], jnp.concatenate([bias_sum, jnp.zeros((1, 640), f32)], axis=1), jnp.zeros((14, 768), f32)], axis=0
    )
    for r in range(4):
        half[r, 192:208, :] = extra.astype(bf16)

    lane = lax.broadcasted_iota(jnp.int32, (TROWS, 128), 1)
    here, before = gp[16 : 16 + TROWS, :], gp[15 : 15 + TROWS, :]
    a, b = pair_slots(x_ref.at[pair], 1920)
    p0[...] = a
    p1[...] = b
    pack0, pack1 = gather_slots((256, 384), 0), gather_slots((256, 384), 192)
    for j in range(2):
        bb[0:16, :] = jnp.zeros((16, 128), f32)
        if j == 0:
            bb[16 : 16 + TROWS, :] = jnp.where(lane < 64, here, pltpu.roll(before, 64, 1))
        else:
            bb[16 : 16 + TROWS, :] = jnp.where(lane < 64, pltpu.roll(here, 64, 1), before)
        for p in range(8):
            g2[:, 128 * p : 128 * p + 128] = bb[16 - 2 * p : 16 - 2 * p + TROWS, :].astype(bf16)
        slots = (p0, p1)[j]
        for q in range(4):
            xt[128 * q : 128 * q + 128, :] = slots[32 * q : 32 * q + TROWS, :].astype(f32).T.astype(bf16)
        for side in range(2):
            base = 512 * side
            left = mm(xt[...], g2[:, base : base + 256]).astype(bf16)
            right = mm(xt[...], g2[:, base + 256 : base + 512]).astype(bf16)
            packed = (mm(left, pack0) + mm(right, pack1)).astype(bf16)
            for m in range(4):
                tile = jnp.concatenate([packed[128 * m : 128 * m + 48], packed[128 * m + 64 : 128 * m + 112]], axis=0)
                half[xor2(me, m), 96 * j : 96 * j + 96, 384 * side : 384 * side + 384] = tile


def conv_sync_kernel(
    gsum, pre_ref, x_ref, sums_ref, wd_ref, xu, a_ref, b_ref,
    fu, fa, fb, fc, ou, oa, ob, oc, f0, f1, f2, f3,
    gp, p0, p1, bb, g2, xt, y_ref, t_ref, gf, g, fg, s1, s2, s3,
    csend, ckeep, cgot, ra, rb, rc, xa, xb, eu, ea, eb, ec, yu, ya, yb, yc,
    ss, so, re, rr, sc, rcv, wide_s, wide_r, core_s, core_r,
):
    n, me = lax.axis_index("narrow"), lax.axis_index("wide")
    z, core = n // 2, n % 2
    MESH = pl.DeviceIdType.MESH

    def copy(src, dst, send, recv, device):
        return pltpu.make_async_remote_copy(
            src_ref=src, dst_ref=dst, send_sem=send, recv_sem=recv, device_id=device, device_id_type=MESH
        )

    def along(zz, cc=core):
        return (2 * zz + cc, me)

    barrier = pltpu.get_barrier_semaphore()

    def greet(device):
        pl.semaphore_signal(barrier, inc=1, device_id=device, device_id_type=MESH)

    for r in range(1, 4):
        greet((n, xor2(me, r)))
    greet(along(z, 1 - core))

    @pl.when(z > 0)
    def _():
        greet(along(z - 1))

    @pl.when(z < 3)
    def _():
        greet(along(z + 1))

    pl.semaphore_wait(barrier, 4 + jnp.minimum(z, 1) + jnp.minimum(3 - z, 1))

    def over_wide(which, r, src, dst):
        return copy(src, dst, wide_s.at[3 * which + r - 1], wide_r.at[3 * which + r - 1], (n, xor2(me, r)))

    send_b = [over_wide(0, r, b_ref.at[r], rb.at[r - 1]) for r in (3, 1, 2)]
    send_a = [over_wide(1, r, a_ref.at[r], ra.at[r - 1]) for r in (3, 1, 2)]
    for c in send_b + send_a:
        c.start()

    pieces = [(3, None, 96 * r, 96) for r in range(4)]
    pieces += [(0, r, 0, 96) for r in range(4)] + [(1, None, 128 * r, 128) for r in range(4)]
    for r in range(4):
        pieces += [(2, r, 0, 112), (2, r, 112, 96)]
    count = len(pieces)
    set_u, set_b, set_a, set_c = range(0, 4), range(4, 8), range(8, 12), range(12, count)

    def views(refs):
        out = []
        for which, r, row, rows in pieces:
            ref = refs[which]
            out.append(ref.at[row : row + rows] if r is None else ref.at[r, row : row + rows])
        return out

    x, e, y, f, o = (views(refs) for refs in ((xb, xa, csend, xu), (eb, ea, ec, eu), (yb, ya, yc, yu), (fb, fa, fc, fu), (ob, oa, oc, ou)))

    def first(k, here):
        return k % 2 == (0 if here == 1 else 1)

    def swap(k):
        return copy(f[k], o[k], sc.at[k], rcv.at[k], along(z, 1 - core))

    def inward(k, here):
        return copy(x[k], e[k], ss.at[k], re.at[k], along(1 if here == 0 else 2))

    def across(k, here):
        src = y[k] if first(k, here) else f[k]
        return copy(src, src, ss.at[k], rr.at[k], along(3 - here))

    def outward(k, here):
        return copy(f[k], f[k], so.at[k], rr.at[k], along(0 if here == 1 else 3))

    def at_ends(do):
        pl.when(z == 0)(lambda: do(0))
        pl.when(z == 3)(lambda: do(3))

    def at_inner(do):
        pl.when(z == 1)(lambda: do(1))
        pl.when(z == 2)(lambda: do(2))

    def begin(ks):
        def do(here):
            for k in ks:
                inward(k, here).start()

        at_ends(do)

    def meet(ks, here):
        for k in ks:
            inward(k, here).wait_recv()
            if first(k, here):
                y[k][...] = (x[k][...].astype(f32) + e[k][...].astype(f32)).astype(bf16)
                across(k, here).start()

    def close(ks, here):
        for k in ks:
            if not first(k, here):
                across(k, here).wait_recv()
                f[k][...] = (x[k][...].astype(f32) + e[k][...].astype(f32) + y[k][...].astype(f32)).astype(bf16)
                across(k, here).start()
                outward(k, here).start()
                swap(k).start()

    def pass_on(ks, here):
        for k in ks:
            if first(k, here):
                across(k, here).wait_recv()
                outward(k, here).start()
                swap(k).start()

    def wgrad(pair, half, slot):
        wgrad_pair(
            pair, me, gsum, pre_ref, x_ref, sums_ref, half, gf.at[slot], g.at[slot],
            gp, p0, p1, bb, g2, xt,
        )

    def dgrad(pair, slot):
        a, b = pair_slots(g.at[slot], 1920)
        p0[...] = a
        p1[...] = b
        value = conv_block((p0, p1), wd_ref.at[pl.ds(2 * pair, 2)], y_ref, t_ref, 1) + gf[slot]
        fg[pair] = value.astype(bf16)

    begin(set_u)
    wgrad(1 - core, csend, 0)
    to_core = copy(csend, cgot, core_s, core_r, along(z, 1 - core))
    to_core.start()
    for c in send_b:
        c.wait()
    xb[0] = b_ref[0]
    for r in range(1, 4):
        xb[r] = rb[r - 1]
    begin(set_b)
    at_inner(lambda here: meet(set_u, here))

    wgrad(core, ckeep, 1)
    to_core.wait()
    for r in range(4):
        ckeep[r] = (ckeep[r].astype(f32) + cgot[r].astype(f32)).astype(bf16)
    send_c = [over_wide(2, r, ckeep.at[r], rc.at[r - 1]) for r in (3, 1, 2)]
    for c in send_c:
        c.start()

    def inner_b(here):
        close(set_u, here)
        meet(set_b, here)

    at_inner(inner_b)
    dgrad(1 - core, 0)

    def inner_c(here):
        pass_on(set_u, here)
        close(set_b, here)

    at_inner(inner_c)
    for c in send_a:
        c.wait()
    xa[...] = (a_ref[0].astype(f32) + ra[0].astype(f32) + ra[1].astype(f32) + ra[2].astype(f32)).astype(bf16)
    begin(set_a)
    dgrad(core, 1)
    pack0, pack1 = gather_slots((256, 384), 0), gather_slots((256, 384), 192)

    def rows_of(lo, rows):
        return jnp.concatenate([fg[0, lo : lo + rows, :], fg[1, lo : lo + rows, :]], axis=1)

    outs = (f0, s1, s2, s3)
    for d in range(4):
        low = jnp.concatenate([rows_of(FR * d + 256, 128), rows_of(SBASE, 128)], axis=0)
        chunk = (mm(rows_of(FR * d, 256), pack0) + mm(low, pack1)).astype(bf16)
        for r in range(4):

            @pl.when(xor2(me, d) == r)
            def _():
                outs[r][...] = chunk

    for c in send_c:
        c.wait()
    csend[0] = ckeep[0]
    for r in range(1, 4):
        csend[r] = rc[r - 1]
    begin(set_c)
    send_f = [over_wide(3, r, (s1, s2, s3)[r - 1], (f1, f2, f3)[r - 1]) for r in (3, 1, 2)]
    for c in send_f:
        c.start()

    def inner(here):
        pass_on(set_b, here)
        rest = list(set_a) + list(set_c)
        for i in range(0, len(rest), 2):
            pair = rest[i : i + 2]
            meet(pair, here)
            close(pair, here)
            if i:
                pass_on(rest[i - 2 : i], here)
        pass_on(rest[-2:], here)
        for k in range(count):
            across(k, here).wait_send()
            outward(k, here).wait_send()
            swap(k).wait()

    def outer(here):
        for k in range(count):
            copy(f[k], f[k], so.at[k], rr.at[k], along(z)).wait_recv()
            swap(k).start()
        for k in range(count):
            inward(k, here).wait_send()
            swap(k).wait()

    at_inner(inner)
    at_ends(outer)
    for c in send_f:
        c.wait()


def conv_sync(gsum, pre, xp, sums, wd, up_sum, ffn_halves, qkv_halves):
    sds = jax.ShapeDtypeStruct
    shapes = [(384, 768), (512, 768), (4, 96, 768), (4, 208, 768)]
    sem = pltpu.SemaphoreType.DMA
    return pl.pallas_call(
        conv_sync_kernel,
        in_specs=[vmem()] * 8,
        out_specs=[vmem()] * 12,
        out_shape=[sds(v, bf16) for v in shapes * 2] + [sds((256, 384), bf16)] * 4,
        scratch_shapes=[
            pltpu.VMEM((16 + TROWS, 128), f32),
            pltpu.VMEM((1920, 128), bf16),
            pltpu.VMEM((1920, 128), bf16),
            pltpu.VMEM((16 + TROWS, 128), f32),
            pltpu.VMEM((TROWS, 1024), bf16),
            pltpu.VMEM((512, TROWS), bf16),
            pltpu.VMEM((CB + 16, 1024), f32),
            pltpu.VMEM((CB + 8, 128), f32),
            pltpu.VMEM((2, TROWS, 128), f32),
            pltpu.VMEM((2, 1936, 128), bf16),
            pltpu.VMEM((2, TROWS, 128), bf16),
        ]
        + [pltpu.VMEM((256, 384), bf16)] * 3
        + [pltpu.VMEM((4, 208, 768), bf16)] * 3
        + [pltpu.VMEM((3, 512, 768), bf16), pltpu.VMEM((3, 96, 768), bf16), pltpu.VMEM((3, 208, 768), bf16)]
        + [pltpu.VMEM((512, 768), bf16), pltpu.VMEM((4, 96, 768), bf16)]
        + [pltpu.VMEM(v, bf16) for v in shapes * 2]
        + [sem((20,))] * 6
        + [sem((12,)), sem((12,)), sem, sem],
        compiler_params=params(collective_id=1, has_side_effects=True),
        cost_estimate=cost(100),
        name="conv_sync",
    )(gsum, pre, xp, sums, wd, up_sum, ffn_halves, qkv_halves)


def unpack_frames_kernel(s_ref, c0, c1, c2, c3, o_ref):
    me, li = s_ref[0], s_ref[1]
    r_i, c_i = iota2((256, 768))
    top = jnp.zeros((256, 768), f32)
    low = jnp.zeros((256, 768), f32)
    for r, chunk in enumerate((c0, c1, c2, c3)):
        base = 192 * (me ^ r)
        inside = (c_i >= base) & (c_i < base + 192)
        top += mm(chunk[:, 0:256], ((c_i - base == r_i) & inside).astype(f32).astype(bf16))
        low += mm(chunk[:, 128:384], ((c_i - base == r_i - 64) & inside).astype(f32).astype(bf16))
    o_ref[li, 0:256, :] = top.astype(bf16)
    o_ref[li, 256:384, :] = low[0:128].astype(bf16)
    slot = me * FR + lax.broadcasted_iota(jnp.int32, (128, 768), 0)
    o_ref[1 - li, 0:128, :] = jnp.where(slot < SHORT, low[128:], 0.0).astype(bf16)
    o_ref[1 - li, 128:384, :] = jnp.zeros((256, 768), bf16)


def unpack_frames(scal, chunks):
    return pl.pallas_call(
        unpack_frames_kernel,
        in_specs=[smem()] + [vmem()] * 4,
        out_specs=vmem(),
        out_shape=jax.ShapeDtypeStruct((2, FR, 768), bf16),
        compiler_params=params(),
        cost_estimate=cost(3),
        name="unpack_frames",
    )(scal, *chunks)


def kernel_out_kernel(s_ref, own_ref, other_ref, o_ref, small_ref):
    core = s_ref[2]
    for g in range(4):
        half, row = g >> 1, 96 * (g & 1)
        x = jnp.where(half == core, own_ref[0, row : row + 96], other_ref[0, row : row + 96]).astype(f32)
        for k2 in range(2):
            for b in range(16):
                o_ref[16 * k2 + b, g] = x[48 * k2 : 48 * k2 + 48, 48 * b : 48 * b + 48]

    @pl.when(pl.program_id(0) == s_ref[0])
    def _():
        for half in range(2):
            small_ref[half] = jnp.where(half == core, own_ref[0, 192:208], other_ref[0, 192:208])


def kernel_out(scal, own, other):
    return pl.pallas_call(
        kernel_out_kernel,
        grid_spec=pltpu.PrefetchScalarGridSpec(
            num_scalar_prefetch=1,
            grid=(4,),
            in_specs=[pl.BlockSpec((1, 208, 768), lambda i, s: (i ^ s[0], 0, 0))] * 2,
            out_specs=[
                pl.BlockSpec((32, 4, 48, 48), lambda i, s: (0, i, 0, 0)),
                pl.BlockSpec((2, 16, 768), lambda i, s: (0, 0, 0)),
            ],
        ),
        out_shape=[jax.ShapeDtypeStruct((32, 16, 48, 48), f32), jax.ShapeDtypeStruct((2, 16, 768), bf16)],
        compiler_params=params(),
        cost_estimate=cost(9),
        name="kernel_grad_out",
    )(scal, own, other)


def norm(v):
    center = v - jnp.mean(v, axis=-1, keepdims=True)
    scale = lax.rsqrt(jnp.mean(center * center, axis=-1, keepdims=True) + eps_norm)
    return center * scale, scale


def norm_back(e, n, scale):
    return (e - jnp.mean(e, axis=-1, keepdims=True) - n * jnp.mean(e * n, axis=-1, keepdims=True)) * scale


def ffn_kernel(
    s_ref, rows_ref, m0, m1, m2, m3, wo, wu_hbm, bu, wd_hbm, vecs, og,
    lo, ul_hbm, gu_hbm, nl, gd, gac, x0, x1, x2, x3, gst, sums,
    wu, wd, ul, gu, slope, v, gsc, mix, sems,
):
    me, li = s_ref[0], s_ref[1]
    const = FR + UNIQUE
    bo, g1, s1, bd, g2, s2 = (vecs[k : k + 1, :] for k in range(6))
    loads = [
        pltpu.make_async_copy(wu_hbm, wu, sems.at[0]),
        pltpu.make_async_copy(wd_hbm, wd, sems.at[1]),
    ]
    for load in loads:
        load.start()

    def total(x):
        return jnp.sum(x, axis=0, keepdims=True)

    for r, m in enumerate((m0, m1, m2, m3)):
        mix[pl.ds(pl.multiple_of(192 * (me ^ r), 64), 192), :] = m[...]
    out = tn(mix[...], wo[...])
    gsc[0:576, :] = rows_ref[...].astype(f32) + out[0:576] + bo
    last = gsc[const : const + 1, :]
    v[0:FR, :] = gsc[0:FR, :]
    v[FR : FR + 128, :] = jnp.where(me == 0, gsc[FR : FR + 128, :], last)
    mine = jnp.where(me == 0, 1.0, 0.0)
    keep_low = (lax.broadcasted_iota(jnp.int32, (64, 768), 0) < UNIQUE - 128).astype(f32) * mine
    v[FR + 128 : FR + 192, :] = jnp.where(keep_low > 0.5, gsc[FR + 128 : FR + 192, :], last)
    v[FR + 192 :, :] = jnp.broadcast_to(last, (192, 768))

    n1, scale1 = norm(v[...])
    v[...] = n1
    norm_one = n1 * g1 + s1
    low = norm_one.astype(bf16)
    nl[...] = low
    down = norm_one + bd
    stores = []
    loads[0].wait()
    for j in range(4):
        cols = slice(768 * j, 768 * j + 768)
        up = mm(low, wu[:, cols]) + bu[:, cols]
        cdf = gelu_parts(up)
        slope[:, cols] = cdf + up * density(up)
        act = (up * cdf).astype(bf16)
        ul[:, cols] = act
        stores.append(pltpu.make_async_copy(ul.at[:, cols], ul_hbm.at[:, cols], sems.at[2 + j]))
        stores[-1].start()
        if j == 0:
            loads[1].wait()
        down += mm(act, wd[cols, :])
    n2, scale2 = norm(down)
    result = (n2 * g2 + s2).astype(bf16)
    lo[li] = result[0:FR]
    lo[1 - li] = result[FR:]
    given = jnp.concatenate([og[li], og[1 - li]], axis=0).astype(f32)
    sums[8:9, :] = total(given * n2)
    sums[9:10, :] = total(given)
    sums[10:16, :] = jnp.zeros((6, 768), f32)
    grad_two = norm_back(given * g2, n2, scale2)
    grad_down = grad_two.astype(bf16)
    gd[...] = grad_down
    sums[7:8, :] = total(grad_down.astype(f32))
    grad_n = grad_two
    for j in range(4):
        cols = slice(768 * j, 768 * j + 768)
        grad_up = (mm_nt(grad_down, wd[cols, :]) * slope[:, cols]).astype(bf16)
        gu[:, cols] = grad_up
        stores.append(pltpu.make_async_copy(gu.at[:, cols], gu_hbm.at[:, cols], sems.at[6 + j]))
        stores[-1].start()
        sums[j : j + 1, :] = total(grad_up.astype(f32))
        grad_n += mm_nt(grad_up, wu[:, cols])
    n1 = v[...]
    sums[5:6, :] = total(grad_n * n1)
    sums[6:7, :] = total(grad_n)
    grad_one = norm_back(grad_n * g1, n1, scale1)
    grad_attn = grad_one.astype(bf16).astype(f32)
    sums[4:5, :] = total(grad_attn)

    at = lax.broadcasted_iota(jnp.int32, (64, 768), 0) == UNIQUE - 128

    def collapsed(g):
        upper = g[FR : FR + 128] * mine
        lower = g[FR + 128 : FR + 192] * keep_low
        rest = total(g[FR:]) - total(upper) - total(lower)
        return jnp.concatenate(
            [g[0:FR], upper, jnp.where(at, rest, lower), jnp.zeros((64, 768), f32)], axis=0
        )

    gac[...] = collapsed(grad_attn).astype(bf16)
    for r, out in enumerate((x0, x1, x2, x3)):
        at_r = pl.ds(pl.multiple_of(192 * (me ^ r), 64), 192)
        out[...] = mm_nt(wo[at_r, :], gac[...]).astype(bf16)
    gsc[...] = collapsed(grad_one)
    gst[...] = gsc[...].T.astype(bf16)
    for store in stores:
        store.wait()


def ffn(scal, rows, mix, wo, wu, bu, wd, vecs, og):
    sds = jax.ShapeDtypeStruct
    hbm = pl.BlockSpec(memory_space=pl.ANY)
    return pl.pallas_call(
        ffn_kernel,
        in_specs=[smem()] + [vmem()] * 6 + [hbm, vmem(), hbm, vmem(), vmem()],
        out_specs=[vmem(), hbm, hbm] + [vmem()] * 9,
        out_shape=[
            sds((2, FR, 768), bf16), sds((768, 3072), bf16), sds((768, 3072), bf16), sds((768, 768), bf16),
            sds((768, 768), bf16), sds((640, 768), bf16),
        ]
        + [sds((CH, 640), bf16)] * 4
        + [sds((768, 640), bf16), sds((16, 768), f32)],
        scratch_shapes=[
            pltpu.VMEM((768, 3072), bf16),
            pltpu.VMEM((3072, 768), bf16),
            pltpu.VMEM((768, 3072), bf16),
            pltpu.VMEM((768, 3072), bf16),
            pltpu.VMEM((768, 3072), f32),
            pltpu.VMEM((768, 768), f32),
            pltpu.VMEM((640, 768), f32),
            pltpu.VMEM((768, 640), bf16),
            pltpu.SemaphoreType.DMA((10,)),
        ],
        compiler_params=params(),
        cost_estimate=cost(28),
        name="ffn",
    )(scal, rows, *mix, wo, wu, bu, wd, vecs, og)


def tn(a, b):
    return lax.dot_general(a, b, (((0,), (0,)), ((), ())), preferred_element_type=f32)


def finish_kernel(s_ref, own1, other1, own2, other2, ownb, otherb, up, down, out, wq, wk, wv, small, a1, a2, b_ref):
    me, core = s_ref[0], s_ref[2]
    for buf, own, other in ((a1, own1, other1), (a2, own2, other2)):
        buf[core] = own[...]
        buf[1 - core] = other[...]
    b_ref[:, pl.ds(pl.multiple_of(96 * core, 32), 96), :] = ownb[...]
    b_ref[:, pl.ds(pl.multiple_of(96 - 96 * core, 32), 96), :] = otherb[...]
    for j in range(4):
        row = 192 * (j & 1)
        up[:, 768 * j : 768 * j + 768] = a1[j >> 1, row : row + 192, :].astype(f32)
    down[0:512, :] = a2[0].astype(f32)
    down[512:768, :] = a2[1, 0:256, :].astype(f32)
    out[...] = a2[1, 256:448, :].astype(f32)
    small[...] = a2[1, 448:464, :].astype(f32)
    r_i, c_i = iota2((256, 768))
    totals = [jnp.zeros((CH, 768), f32)] * 3
    for r in range(4):
        base = 192 * (me ^ r)
        hit = (c_i - base == r_i) & (r_i < 192)
        move = hit.astype(f32).astype(bf16)
        for k in range(3):
            totals[k] = totals[k] + mm(b_ref[r, :, 256 * k : 256 * k + 256], move)
    wq[...], wk[...], wv[...] = totals


def finish(scal, *parts):
    sds = jax.ShapeDtypeStruct
    return pl.pallas_call(
        finish_kernel,
        in_specs=[smem()] + [vmem()] * 6,
        out_specs=[vmem()] * 7,
        out_shape=[sds((CH, 3072), f32), sds((768, 768), f32)] + [sds((CH, 768), f32)] * 4 + [sds((16, 768), f32)],
        scratch_shapes=[
            pltpu.VMEM((2, 384, 768), bf16),
            pltpu.VMEM((2, 512, 768), bf16),
            pltpu.VMEM((4, CH, 768), bf16),
        ],
        compiler_params=params(),
        cost_estimate=cost(6),
        name="weight_grads_out",
    )(scal, *parts)


def on_device(
    frames_in, lengths, kernel, conv_bias, w_query, b_query, w_key, w_value, b_value, w_out, b_out,
    gain_one, shift_one, w_up, b_up, w_down, b_down, gain_two, shift_two, out_grad,
):
    me = lax.axis_index("wide").astype(jnp.int32)
    place_n = lax.axis_index("narrow").astype(jnp.int32)
    core, z = place_n & 1, place_n >> 1
    li = jnp.where(lengths[0] >= lengths[1], 0, 1).astype(jnp.int32)
    scal = jnp.stack([me, li, core, z])
    chunks = pack_frames(scal, frames_in)
    vec = jnp.concatenate([jnp.stack([conv_bias, b_query, b_value]), jnp.zeros((13, conv_bias.shape[0]), bf16)], axis=0)
    vecs = jnp.stack([b_out, gain_one, shift_one, b_down, gain_two, shift_two]).astype(f32)
    bu = b_up.astype(f32)[None]

    wd, pre, xp, h0, h1, h2, h3, qkv, mixed_t, lse, rows, wqkv, *mix = front_sync(
        chunks, kernel, vec, w_query, w_key, w_value
    )
    first = [h0, h1, h2, h3]
    layer_out, ul, gu, nl, gd, gac, x0, x1, x2, x3, gst, sums = ffn(
        scal, rows, mix, w_out, w_up, bu, w_down, vecs, out_grad
    )
    up_sum, ffn_halves, qkv_halves, gsum, qkv_sums = attn_sync(
        qkv, mixed_t, lse, [x0, x1, x2, x3], gst, wqkv, first, nl, gd, ul, gu, mix, gac, sums
    )
    own1, own2, ownb, ownc, other1, other2, otherb, otherc, *fchunks = conv_sync(
        gsum, pre, xp, qkv_sums, wd, up_sum, ffn_halves, qkv_halves
    )
    frames_grad = unpack_frames(scal, fchunks)
    up, down, out, wq, wk, wv, small = finish(scal, own1, other1, own2, other2, ownb, otherb)
    grad_kernel, tiny = kernel_out(scal, ownc, otherc)
    tiny = tiny.astype(f32)

    def mine(row):
        return lax.dynamic_slice_in_dim(small[row], me * CH, CH, axis=0)

    bias_grad = jnp.concatenate([tiny[0, 1, :128], tiny[1, 1, :128]]).reshape(4, 64)[:, :48].reshape(CH)
    grad_b_up = lax.dynamic_index_in_dim(small[:4], me, 0, keepdims=False)
    return (
        layer_out,
        frames_grad,
        grad_kernel,
        bias_grad,
        wq,
        tiny[0, 0, 0:192],
        wk,
        wv,
        tiny[0, 0, 512:704],
        out,
        mine(4),
        mine(5),
        mine(6),
        up,
        grad_b_up,
        down,
        mine(7),
        mine(8),
        mine(9),
    )


def with_halo(x, sides, width):
    for axis, dim in sides:
        count, length = (lax.axis_size(axis), x.shape[dim])
        up = [(i, (i + 1) % count) for i in range(count - 1)]
        down = [(j, i) for i, j in up]
        last = lax.slice_in_dim(x, length - width, length, axis=dim)
        initial = lax.slice_in_dim(x, 0, width, axis=dim)
        before = lax.ppermute(last, axis, up)
        after = lax.ppermute(initial, axis, down)
        x = jnp.concatenate([before, x, after], axis=dim)
    return x


def layer_norm(value, gain, shift):
    center = value - jnp.mean(value, axis=-1, keepdims=True)
    spread = jnp.mean(center * center, axis=-1, keepdims=True)
    return center * lax.rsqrt(spread + eps_norm) * gain + shift


def gelu_exact(value):
    return jax.nn.gelu(value, approximate=False)


def project(rows_in, weight):
    return jnp.einsum("cfd,de->cfe", rows_in, weight, preferred_element_type=jnp.float32)


def project_back(grad_in, weight):
    return jnp.einsum("cfe,de->cfd", grad_in, weight, preferred_element_type=jnp.float32)


def weight_grad(rows_in, grad_in):
    return jnp.einsum("cfd,cfe->de", rows_in, grad_in, preferred_element_type=jnp.float32)


def row_total(grad_in):
    return jnp.sum(grad_in.astype(jnp.float32), axis=(0, 1))


def head_view(rows_in):
    return rows_in.reshape(rows_in.shape[0], rows_in.shape[1], HEADS, rows_in.shape[2] // HEADS)


def conv_apply(padded, weight, frames):
    kernel_span, groups, inner_ch, outer_ch = weight.shape
    taps_weight = jnp.transpose(weight, (0, 2, 1, 3)).reshape(
        kernel_span, inner_ch, groups * outer_ch
    )
    result = lax.conv_general_dilated(
        padded,
        taps_weight,
        (1,),
        "VALID",
        dimension_numbers=("NWC", "WIO", "NWC"),
        feature_group_count=groups,
        preferred_element_type=jnp.float32,
    )
    return result[:, :frames, :]


def conv_weight_grad(padded, grad_in, kernel_shape):
    kernel_span, groups, inner_ch, outer_ch = kernel_shape
    result = lax.conv_general_dilated(
        padded,
        grad_in,
        (1,),
        "VALID",
        dimension_numbers=("CWN", "IWO", "NWC"),
        batch_group_count=groups,
        preferred_element_type=jnp.float32,
    )
    result = result[:, :kernel_span, :].reshape(inner_ch, kernel_span, groups, outer_ch)
    return jnp.transpose(result, (1, 2, 0, 3))


def key_valid_at(lengths, first_row, row_count):
    return (first_row + jnp.arange(row_count, dtype=jnp.int32))[None, :] < lengths[:, None]


def masked_scores(query_h, keys_h, valid_keys, score_scale):
    scores = (
        jnp.einsum("cqhd,ckhd->cqhk", query_h, keys_h, preferred_element_type=jnp.float32)
        * score_scale
    )
    return jnp.where(valid_keys[:, None, None, :], scores, neg_large)


def block_terms(query_h, grad_h, lse_rows, delta_rows, keys_h, values_h, valid_keys, score_scale):
    scores = masked_scores(query_h, keys_h, valid_keys, score_scale)
    probs = jnp.where(valid_keys[:, None, None, :], jnp.exp(scores - lse_rows[..., None]), 0.0)
    grad_probs = jnp.einsum("cqhd,ckhd->cqhk", grad_h, values_h, preferred_element_type=jnp.float32)
    grad_scores = (probs * (grad_probs - delta_rows[..., None])).astype(jnp.bfloat16)
    results = []
    results.append(
        jnp.einsum("cqhk,ckhd->cqhd", grad_scores, keys_h, preferred_element_type=jnp.float32)
        * score_scale
    )
    results.append(
        jnp.einsum("cqhk,cqhd->ckhd", grad_scores, query_h, preferred_element_type=jnp.float32)
        * score_scale
    )
    results.append(
        jnp.einsum(
            "cqhk,cqhd->ckhd",
            probs.astype(jnp.bfloat16),
            grad_h,
            preferred_element_type=jnp.float32,
        )
    )
    return tuple(results)


def on_device_any(
    frames_in,
    lengths,
    kernel,
    conv_bias,
    w_query,
    b_query,
    w_key,
    w_value,
    b_value,
    w_out,
    b_out,
    gain_one,
    shift_one,
    w_up,
    b_up,
    w_down,
    b_down,
    gain_two,
    shift_two,
    out_grad,
):
    clip_count, frames, width = frames_in.shape
    head_dim = width // HEADS
    score_scale = head_dim ** (-0.5)
    half_span = kernel.shape[0] // 2
    wide_size = lax.axis_size("wide")
    positions = lax.axis_index("wide") * frames + jnp.arange(frames, dtype=jnp.int32)
    frame_valid = positions[None, :] < lengths[:, None]
    masked = jnp.where(frame_valid[..., None], frames_in, jnp.zeros((), jnp.bfloat16))
    padded = with_halo(masked, (("wide", 1),), half_span)
    pre_act = conv_apply(padded, kernel, frames) + conv_bias.astype(jnp.float32)
    first_act, pull_first = jax.vjp(gelu_exact, pre_act)
    first_out = masked.astype(jnp.float32) + first_act
    first_low = first_out.astype(jnp.bfloat16)
    query_rows = (project(first_low, w_query) + b_query.astype(jnp.float32)).astype(jnp.bfloat16)
    key_rows = project(first_low, w_key).astype(jnp.bfloat16)
    value_rows = (project(first_low, w_value) + b_value.astype(jnp.float32)).astype(jnp.bfloat16)
    query_h = head_view(query_rows)
    per_step = max(1, min(wide_size, 512 // frames))
    while wide_size % per_step:
        per_step -= 1
    run_max = jnp.full((clip_count, frames, HEADS), neg_large, jnp.float32)
    run_acc = jnp.zeros((clip_count, frames, HEADS, head_dim), jnp.float32)
    keys_p = lax.all_gather(key_rows, "wide", axis=1, tiled=True)
    values_p = lax.all_gather(value_rows, "wide", axis=1, tiled=True)
    row_count = keys_p.shape[1]
    valid_keys = key_valid_at(lengths, jnp.int32(0), row_count)
    scores = masked_scores(query_h, head_view(keys_p), valid_keys, score_scale)
    new_max = jnp.maximum(run_max, jnp.max(scores, axis=-1))
    weights = jnp.where(valid_keys[:, None, None, :], jnp.exp(scores - new_max[..., None]), 0.0)
    factor = jnp.exp(run_max - new_max)
    run_sum = jnp.sum(weights, axis=-1)
    run_acc = run_acc * factor[..., None] + jnp.einsum(
        "cqhk,ckhd->cqhd",
        weights.astype(jnp.bfloat16),
        head_view(values_p),
        preferred_element_type=jnp.float32,
    )
    run_max, run_sum, run_acc = (new_max, run_sum, run_acc)
    lse_rows = run_max + jnp.log(run_sum)
    mixed_heads = run_acc / run_sum[..., None]
    mixed_low = mixed_heads.reshape(clip_count, frames, width).astype(jnp.bfloat16)
    attn_out = project(mixed_low, w_out) + b_out.astype(jnp.float32)
    sum_one = first_out + attn_out
    norm_one, pull_one = jax.vjp(
        layer_norm, sum_one, gain_one.astype(jnp.float32), shift_one.astype(jnp.float32)
    )
    norm_low = norm_one.astype(jnp.bfloat16)
    up_pre = project(norm_low, w_up) + b_up.astype(jnp.float32)
    up_act, pull_up = jax.vjp(gelu_exact, up_pre)
    up_low = up_act.astype(jnp.bfloat16)
    down_out = project(up_low, w_down) + b_down.astype(jnp.float32)
    sum_two = norm_one + down_out
    layer_out, pull_two = jax.vjp(
        layer_norm, sum_two, gain_two.astype(jnp.float32), shift_two.astype(jnp.float32)
    )
    grad_sum_two, grad_gain_two, grad_shift_two = pull_two(out_grad.astype(jnp.float32))
    grad_down = grad_sum_two.astype(jnp.bfloat16)
    grad_w_down = weight_grad(up_low, grad_down)
    grad_b_down = row_total(grad_down)
    grad_up = pull_up(project_back(grad_down, w_down))[0].astype(jnp.bfloat16)
    grad_w_up = weight_grad(norm_low, grad_up)
    grad_b_up = row_total(grad_up)
    grad_norm_one = grad_sum_two + project_back(grad_up, w_up)
    grad_sum_one, grad_gain_one, grad_shift_one = pull_one(grad_norm_one)
    grad_attn = grad_sum_one.astype(jnp.bfloat16)
    grad_w_out = weight_grad(mixed_low, grad_attn)
    grad_b_out = row_total(grad_attn)
    grad_mixed = project_back(grad_attn, w_out).astype(jnp.bfloat16)
    grad_h = head_view(grad_mixed)
    delta_rows = jnp.sum(grad_h.astype(jnp.float32) * mixed_heads, axis=-1)
    total_slots = wide_size * frames
    first_row = jnp.int32(0)
    grad_q = jnp.zeros((clip_count, frames, HEADS, head_dim), jnp.float32)
    grad_k_all = jnp.zeros((clip_count, total_slots, width), jnp.float32)
    grad_v_all = jnp.zeros((clip_count, total_slots, width), jnp.float32)
    keys_p = lax.all_gather(key_rows, "wide", axis=1, tiled=True)
    values_p = lax.all_gather(value_rows, "wide", axis=1, tiled=True)
    row_count = keys_p.shape[1]
    valid_keys = key_valid_at(lengths, first_row, row_count)
    part_q, part_k, part_v = block_terms(
        query_h,
        grad_h,
        lse_rows,
        delta_rows,
        head_view(keys_p),
        head_view(values_p),
        valid_keys,
        score_scale,
    )
    old_k = lax.dynamic_slice_in_dim(grad_k_all, first_row, row_count, 1)
    old_v = lax.dynamic_slice_in_dim(grad_v_all, first_row, row_count, 1)
    grad_k_all = lax.dynamic_update_slice_in_dim(
        grad_k_all, old_k + part_k.reshape(clip_count, row_count, width), first_row, 1
    )
    grad_v_all = lax.dynamic_update_slice_in_dim(
        grad_v_all, old_v + part_v.reshape(clip_count, row_count, width), first_row, 1
    )
    grad_k_own, grad_v_own = (
        lax.psum_scatter(
            grad_k_all.astype(jnp.bfloat16), "wide", scatter_dimension=1, tiled=True
        ).astype(jnp.float32),
        lax.psum_scatter(
            grad_v_all.astype(jnp.bfloat16), "wide", scatter_dimension=1, tiled=True
        ).astype(jnp.float32),
    )
    grad_q_low = (grad_q + part_q).reshape(clip_count, frames, width).astype(jnp.bfloat16)
    grad_k_low = grad_k_own.astype(jnp.bfloat16)
    grad_v_low = grad_v_own.astype(jnp.bfloat16)
    grad_w_query = weight_grad(first_low, grad_q_low)
    grad_b_query = row_total(grad_q_low)
    grad_w_key = weight_grad(first_low, grad_k_low)
    grad_w_value = weight_grad(first_low, grad_v_low)
    grad_b_value = row_total(grad_v_low)
    grad_first = (
        grad_sum_one
        + project_back(grad_q_low, w_query)
        + project_back(grad_k_low, w_key)
        + project_back(grad_v_low, w_value)
    )
    grad_pre = pull_first(grad_first)[0].astype(jnp.bfloat16)
    grad_conv_bias = row_total(grad_pre)
    grad_kernel = conv_weight_grad(padded, grad_pre, kernel.shape)
    grad_padded = with_halo(grad_pre, (("wide", 1),), half_span)
    flipped = jnp.transpose(kernel[::-1], (0, 1, 3, 2))
    grad_masked = grad_first + conv_apply(grad_padded[:, 1:], flipped, frames)
    frames_grad = jnp.where(frame_valid[..., None], grad_masked, 0.0).astype(jnp.bfloat16)
    shards = (
        lax.psum_scatter(
            grad_kernel.astype(jnp.bfloat16), "wide", scatter_dimension=0, tiled=True
        ).astype(jnp.float32),
        lax.psum_scatter(
            grad_conv_bias.astype(jnp.bfloat16), "wide", scatter_dimension=0, tiled=True
        ).astype(jnp.float32),
        lax.psum_scatter(
            grad_w_query.astype(jnp.bfloat16), "wide", scatter_dimension=0, tiled=True
        ).astype(jnp.float32),
        lax.psum_scatter(
            grad_b_query.astype(jnp.bfloat16), "wide", scatter_dimension=0, tiled=True
        ).astype(jnp.float32),
        lax.psum_scatter(
            grad_w_key.astype(jnp.bfloat16), "wide", scatter_dimension=0, tiled=True
        ).astype(jnp.float32),
        lax.psum_scatter(
            grad_w_value.astype(jnp.bfloat16), "wide", scatter_dimension=0, tiled=True
        ).astype(jnp.float32),
        lax.psum_scatter(
            grad_b_value.astype(jnp.bfloat16), "wide", scatter_dimension=0, tiled=True
        ).astype(jnp.float32),
        lax.psum_scatter(
            grad_w_out.astype(jnp.bfloat16), "wide", scatter_dimension=0, tiled=True
        ).astype(jnp.float32),
        lax.psum_scatter(
            grad_b_out.astype(jnp.bfloat16), "wide", scatter_dimension=0, tiled=True
        ).astype(jnp.float32),
        lax.psum_scatter(
            grad_gain_one.astype(jnp.bfloat16), "wide", scatter_dimension=0, tiled=True
        ).astype(jnp.float32),
        lax.psum_scatter(
            grad_shift_one.astype(jnp.bfloat16), "wide", scatter_dimension=0, tiled=True
        ).astype(jnp.float32),
        lax.psum_scatter(
            grad_w_up.astype(jnp.bfloat16), "wide", scatter_dimension=0, tiled=True
        ).astype(jnp.float32),
        lax.psum_scatter(
            grad_b_up.astype(jnp.bfloat16), "wide", scatter_dimension=0, tiled=True
        ).astype(jnp.float32),
        lax.psum_scatter(
            grad_w_down.astype(jnp.bfloat16), "wide", scatter_dimension=0, tiled=True
        ).astype(jnp.float32),
        lax.psum_scatter(
            grad_b_down.astype(jnp.bfloat16), "wide", scatter_dimension=0, tiled=True
        ).astype(jnp.float32),
        lax.psum_scatter(
            grad_gain_two.astype(jnp.bfloat16), "wide", scatter_dimension=0, tiled=True
        ).astype(jnp.float32),
        lax.psum_scatter(
            grad_shift_two.astype(jnp.bfloat16), "wide", scatter_dimension=0, tiled=True
        ).astype(jnp.float32),
    )
    totals = (
        lax.psum(shards[0].astype(jnp.bfloat16), "narrow").astype(jnp.float32),
        lax.psum(shards[1].astype(jnp.bfloat16), "narrow").astype(jnp.float32),
        lax.psum(shards[2].astype(jnp.bfloat16), "narrow").astype(jnp.float32),
        lax.psum(shards[3].astype(jnp.bfloat16), "narrow").astype(jnp.float32),
        lax.psum(shards[4].astype(jnp.bfloat16), "narrow").astype(jnp.float32),
        lax.psum(shards[5].astype(jnp.bfloat16), "narrow").astype(jnp.float32),
        lax.psum(shards[6].astype(jnp.bfloat16), "narrow").astype(jnp.float32),
        lax.psum(shards[7].astype(jnp.bfloat16), "narrow").astype(jnp.float32),
        lax.psum(shards[8].astype(jnp.bfloat16), "narrow").astype(jnp.float32),
        lax.psum(shards[9].astype(jnp.bfloat16), "narrow").astype(jnp.float32),
        lax.psum(shards[10].astype(jnp.bfloat16), "narrow").astype(jnp.float32),
        lax.psum(shards[11].astype(jnp.bfloat16), "narrow").astype(jnp.float32),
        lax.psum(shards[12].astype(jnp.bfloat16), "narrow").astype(jnp.float32),
        lax.psum(shards[13].astype(jnp.bfloat16), "narrow").astype(jnp.float32),
        lax.psum(shards[14].astype(jnp.bfloat16), "narrow").astype(jnp.float32),
        lax.psum(shards[15].astype(jnp.bfloat16), "narrow").astype(jnp.float32),
        lax.psum(shards[16].astype(jnp.bfloat16), "narrow").astype(jnp.float32),
    )
    return (
        layer_out.astype(jnp.bfloat16),
        frames_grad,
        totals[0],
        totals[1],
        totals[2],
        totals[3],
        totals[4],
        totals[5],
        totals[6],
        totals[7],
        totals[8],
        totals[9],
        totals[10],
        totals[11],
        totals[12],
        totals[13],
        totals[14],
        totals[15],
        totals[16],
    )


def solution(mesh):
    rows = P("narrow", "wide", None)
    placed = (rows, P("narrow")) + (P(),) * 17 + (rows,)
    wide = mesh.shape["wide"]
    fast = wide == 4 and mesh.shape["narrow"] == 8
    return jax.shard_map(
        on_device if fast else on_device_any,
        mesh=mesh,
        in_specs=placed,
        out_specs=(rows, rows)
        + (P("wide", None, None, None), P("wide"), P("wide", None), P("wide"), P("wide", None), P("wide", None))
        + (P("wide"), P("wide", None), P("wide"), P("wide"), P("wide"), P("wide", None), P("wide"))
        + (P("wide", None), P("wide"), P("wide"), P("wide")),
        check_vma=False,
    )
```

profile of v0, /device:TPU:0, one launch (start us, length us, event | category | flops | bytes accessed | tf_op | source)
XLA Modules:
  0.0 329.6 jit_solution(7376994853218568474)
XLA Ops:
  0.7 1.3 fusion.2
  3.3 0.6 pad_add_fusion.s_ref
  3.9 0.0 copy-start.1
  3.9 0.0 copy-start.2
  3.9 0.0 copy-start.3
  3.9 3.4 %pack_frames.1 = (bf16[256,384]{1,0:T(8,128)(2,1)}, bf16[256,384]{1,0:T(8,128)(2,1)}, bf16[256,384]{1,0:T(8,128)(2,1)}, bf16[256,384]{1,0:T(8,128)(2,1)}) custom-call(s32[4]{0:T(128)} %pad_add_fusion.s_ref, bf16[2,384,768]{2,1,0:T(8,128)(2,1)} %x_ref.1), custom_call_target="tpu_custom_call" | custom-call | flops 3000000000 | bytes 10200000 | tf_op jit(solution)/shard_map/pack_frames/pallas_call | solution.py:131
  7.3 0.0 copy-done.1
  7.3 0.0 copy-done.2
  7.3 0.0 copy-done.3
  7.4 0.1 pad.5.clone
  7.5 0.7 maximum_maximum_fusion.vec
  8.1 0.0 copy-start
  8.1 0.0 copy-start.4
  8.1 0.0 copy-start.5
  8.2 0.0 copy-start.6
  8.2 0.0 copy-start.7
  8.2 0.0 copy-start.8
  8.2 0.0 copy-start.9
  8.2 70.5 %front_sync.1 = (bf16[4,512,1024]{2,1,0:T(8,128)(2,1)}, f32[2,1792,128]{2,1,0:T(8,128)}, bf16[2,1936,128]{2,1,0:T(8,128)(2,1)}, bf16[864,384]{1,0:T(8,128)(2,1)}...) custom-call(bf16[256,384]{1,0:T(8,128)(2,1)} %get-tuple-element.77.p, ...), custom_call_target="tpu_custom_call" | custom-call | flops 65000001536 | bytes 221000000 | tf_op jit(solution)/shard_map/front_sync/pallas_call | solution.py:381
  78.7 0.0 copy-done
  78.7 0.6 broadcast_in_dim.11
  79.3 0.0 copy-done.4
  79.4 0.0 copy-done.5
  79.4 0.0 copy-done.6
  79.4 0.0 copy-done.7
  79.4 0.0 copy-done.8
  79.4 0.0 copy-done.9
  79.5 0.6 convert_element_type.7.vecs
  80.1 28.6 %ffn.1 = (bf16[2,384,768]{2,1,0:T(8,128)(2,1)}, bf16[768,3072]{1,0:T(8,128)(2,1)}, bf16[768,3072]{1,0:T(8,128)(2,1)}, bf16[768,768]{1,0:T(8,128)(2,1)}, bf16[768...) custom-call(s32[4]{0:T(128)} %pad_add_fusion.s_ref, ...), custom_call_target="tpu_custom_call" | custom-call | flops 28000000000 | bytes 95200000 | tf_op jit(solution)/shard_map/ffn/pallas_call | solution.py:1132
  108.7 73.2 %attn_sync.1 = (bf16[384,768]{1,0:T(8,128)(2,1)}, bf16[4,512,768]{2,1,0:T(8,128)(2,1)}, bf16[4,96,768]{2,1,0:T(8,128)(2,1)}, f32[192,1792]{1,0:T(8,128)}, f32[1,768]{1,0:T(1,128)}) custom-call(bf16[1792,768]{1,0:T(8,128)(2,1)} %get-tuple-element.87.qkv_ref, f32[192,1792]{1,0:T(8,128)} %get-tuple-element.88.ot_ref, f32[8,1792]{1,0:T(8,128)} %get-tuple-element.89.lse_ref, ...), custom_call_target="tpu_custom_call" | custom-call | flops 89999998976 | bytes 306000000 | tf_op jit(solution)/shard_map/attn_sync/pallas_call | solution.py:619
  181.9 123.4 %conv_sync.1 = (bf16[384,768]{1,0:T(8,128)(2,1)}, bf16[512,768]{1,0:T(8,128)(2,1)}, bf16[4,96,768]{2,1,0:T(8,128)(2,1)}, bf16[4,208,768]{2,1,0:T(8,128)(2,1)}, b...) custom-call(f32[192,1792]{1,0:T(8,128)} %get-tuple-element.106.gsum,, ...), custom_call_target="tpu_custom_call" | custom-call | flops 99999997952 | bytes 340000000 | tf_op jit(solution)/shard_map/conv_sync/pallas_call | solution.py:927
  305.3 3.2 unpack_frames.1
  308.6 7.7 %kernel_grad_out.1 = (f32[32,16,48,48]{3,2,1,0:T(8,128)}, bf16[2,16,768]{2,1,0:T(8,128)(2,1)}) custom-call(s32[4]{0:T(128)} %pad_add_fusion.s_ref, bf16[4,208,768]{2,1,0:T(8,128)(2,1)} %get-tuple-element.118.own_ref, bf16[4,208,768]{2,1,0:T(8,128)(2,1)} %get-tuple-element.119.other_ref), custom_call_target="tpu_custom_call" | custom-call | flops 8999999488 | bytes 30600000 | tf_op jit(solution)/shard_map/kernel_grad_out/pallas_call | solution.py:1003
  316.3 0.8 convert_element_type.8
  317.1 0.1 concatenate.13
  317.2 0.1 concatenate.12
  317.3 0.6 reshape.57
  317.9 6.0 %weight_grads_out.1 = (f32[192,3072]{1,0:T(8,128)}, f32[768,768]{1,0:T(8,128)}, f32[192,768]{1,0:T(8,128)}, f32[192,768]{1,0:T(8,128)}, f32[192,768]{1,0:T(8,128...) custom-call(s32[4]{0:T(128)} %pad_add_fusion.s_ref, bf16[384,768]{1,0:T(8,128)(2,1)} %get-tuple-element.122.own1, ...), custom_call_target="tpu_custom_call" | custom-call | flops 6000000000 | bytes 20400000 | tf_op jit(solution)/shard_map/weight_grads_out/pallas_call | solution.py:1190
  324.0 1.3 fusion.1
  325.2 0.9 fusion
  326.1 0.6 constant_dynamic-slice_fusion.4
  326.8 0.6 constant_dynamic-slice_fusion.2
  327.4 0.7 slice.52
  328.2 0.6 dynamic-slice_reduce_fusion
  328.8 0.6 constant_dynamic-slice_fusion
  (13 shorter events, 0.1 us)
Async XLA Ops:
  3.9 3.4 %copy-start.1 = (bf16[768]{0:T(1024)(128)(2,1)S(1)}, bf16[768]{0:T(1024)(128)(2,1)}, u32[]{:S(2)}) copy-start(bf16[768]{0:T(1024)(128)(2,1)} %param.28) | copy-start | bytes 4612
  3.9 3.5 %copy-start.2 = (bf16[768]{0:T(1024)(128)(2,1)S(1)}, bf16[768]{0:T(1024)(128)(2,1)}, u32[]{:S(2)}) copy-start(bf16[768]{0:T(1024)(128)(2,1)} %param.25) | copy-start | bytes 4612
  3.9 3.5 %copy-start.3 = (bf16[768]{0:T(1024)(128)(2,1)S(1)}, bf16[768]{0:T(1024)(128)(2,1)}, u32[]{:S(2)}) copy-start(bf16[768]{0:T(1024)(128)(2,1)} %param.23) | copy-start | bytes 4612
  8.1 70.6 %copy-start = (bf16[3072]{0:T(1024)(128)(2,1)S(1)}, bf16[3072]{0:T(1024)(128)(2,1)}, u32[]{:S(2)}) copy-start(bf16[3072]{0:T(1024)(128)(2,1)} %param.34) | copy-start | bytes 18436
  8.1 71.2 %copy-start.4 = (bf16[768]{0:T(1024)(128)(2,1)S(1)}, bf16[768]{0:T(1024)(128)(2,1)}, u32[]{:S(2)}) copy-start(bf16[768]{0:T(1024)(128)(2,1)} %param.30) | copy-start | bytes 4612
  8.1 71.2 %copy-start.5 = (bf16[768]{0:T(1024)(128)(2,1)S(1)}, bf16[768]{0:T(1024)(128)(2,1)}, u32[]{:S(2)}) copy-start(bf16[768]{0:T(1024)(128)(2,1)} %param.31) | copy-start | bytes 4612
  8.2 71.2 %copy-start.6 = (bf16[768]{0:T(1024)(128)(2,1)S(1)}, bf16[768]{0:T(1024)(128)(2,1)}, u32[]{:S(2)}) copy-start(bf16[768]{0:T(1024)(128)(2,1)} %param.32) | copy-start | bytes 4612
  8.2 71.2 %copy-start.7 = (bf16[768]{0:T(1024)(128)(2,1)S(1)}, bf16[768]{0:T(1024)(128)(2,1)}, u32[]{:S(2)}) copy-start(bf16[768]{0:T(1024)(128)(2,1)} %param.36) | copy-start | bytes 4612
  8.2 71.3 %copy-start.8 = (bf16[768]{0:T(1024)(128)(2,1)S(1)}, bf16[768]{0:T(1024)(128)(2,1)}, u32[]{:S(2)}) copy-start(bf16[768]{0:T(1024)(128)(2,1)} %param.37) | copy-start | bytes 4612
  8.2 71.3 %copy-start.9 = (bf16[768]{0:T(1024)(128)(2,1)S(1)}, bf16[768]{0:T(1024)(128)(2,1)}, u32[]{:S(2)}) copy-start(bf16[768]{0:T(1024)(128)(2,1)} %param.38) | copy-start | bytes 4612
where the time goes:
time: 333 us; the launch traced here: 330 us
  Pallas kernels  316 us (95%)
  local copies, waits for them, and re-layouts  7.79 us (2%)
    pallas_call x1, Pallas kernels, conv_sync(): pl.pallas_call(conv_sync_kernel, in_specs=[vmem()] * 8, out_specs=[vmem()...  123 us
    pallas_call x1, Pallas kernels, attn_sync(): pl.pallas_call(attn_sync_kernel, in_specs=[vmem()] * 15 + [hbm] * 2 + [vm...  73.2 us
    pallas_call x1, Pallas kernels, front_sync(): pl.pallas_call(front_sync_kernel, in_specs=[vmem()] * 4 + [pl.BlockSpec(m...  70.5 us
    pallas_call x1, Pallas kernels, ffn(): pl.pallas_call(ffn_kernel, in_specs=[smem()] + [vmem()] * 6 + [hbm, vmem(...  28.6 us
    pallas_call x1, Pallas kernels, kernel_out(): pl.pallas_call(kernel_out_kernel, grid_spec=pltpu.PrefetchScalarGridSpec(...  7.7 us

commit v1 on v0

--- a/solution.py
+++ b/solution.py
@@ -161,11 +161,11 @@
         wd_ref[128 * q : 128 * q + 128, :] = z_ref[...].T.astype(bf16)
 
 
-def pair_slots(t_ref, rows):
+def pair_slots(t_ref, rows, groups=(0, 1)):
     wide = jnp.concatenate([t_ref[0:rows, :], t_ref[16 : rows + 16, :]], axis=1)
     r, c = iota2((256, 128))
     out = []
-    for j in range(2):
+    for j in groups:
         hit = ((r < 128) & (c == r - 64 * j) & (c < 64)) | ((r >= 128) & (c - 64 == r - 128 - 64 * j) & (c >= 64))
         out.append(mm(wide, hit.astype(f32).astype(bf16)).astype(bf16))
     return out
@@ -409,12 +409,125 @@
     )(*chunks, jnp.transpose(kernel, (1, 2, 3, 0)), vec, wq, wk, wv)
 
 
+class Line:
+    def __init__(self, place, x, e, y, f, o, ss, so, re, rr, sc, rcv, ready=()):
+        self.n, self.me = place
+        self.ready = ready
+        self.z, self.core = self.n // 2, self.n % 2
+        self.x, self.e, self.y, self.f, self.o = x, e, y, f, o
+        self.ss, self.so, self.re, self.rr, self.sc, self.rcv = ss, so, re, rr, sc, rcv
+
+    def copy(self, src, dst, send, recv, z, core=None):
+        return pltpu.make_async_remote_copy(
+            src_ref=src, dst_ref=dst, send_sem=send, recv_sem=recv,
+            device_id=(2 * z + (self.core if core is None else core), self.me), device_id_type=pl.DeviceIdType.MESH,
+        )
+
+    def first(self, k, here):
+        return k % 2 == (0 if here == 1 else 1)
+
+    def swap(self, k):
+        return self.copy(self.f[k], self.o[k], self.sc.at[k], self.rcv.at[k], self.z, 1 - self.core)
+
+    def inward(self, k, here):
+        return self.copy(self.x[k], self.e[k], self.ss.at[k], self.re.at[k], 1 if here == 0 else 2)
+
+    def across(self, k, here):
+        src = self.y[k] if self.first(k, here) else self.f[k]
+        return self.copy(src, src, self.ss.at[k], self.rr.at[k], 3 - here)
+
+    def outward(self, k, here):
+        return self.copy(self.f[k], self.f[k], self.so.at[k], self.rr.at[k], 0 if here == 1 else 3)
+
+    def at_ends(self, do):
+        pl.when(self.z == 0)(lambda: do(0))
+        pl.when(self.z == 3)(lambda: do(3))
+
+    def at_inner(self, do):
+        pl.when(self.z == 1)(lambda: do(1))
+        pl.when(self.z == 2)(lambda: do(2))
+
+    def begin(self, ks):
+        def do(here):
+            for k in ks:
+                self.inward(k, here).start()
+
+        self.at_ends(do)
+
+    def part(self, k):
+        own = self.x[k][...].astype(f32)
+        return own if k in self.ready else own + self.e[k][...].astype(f32)
+
+    def meet(self, ks, here):
+        for k in ks:
+            if k not in self.ready:
+                self.inward(k, here).wait_recv()
+            if self.first(k, here):
+                self.y[k][...] = self.part(k).astype(bf16)
+                self.across(k, here).start()
+
+    def close(self, ks, here):
+        for k in ks:
+            if not self.first(k, here):
+                self.across(k, here).wait_recv()
+                self.f[k][...] = (self.part(k) + self.y[k][...].astype(f32)).astype(bf16)
+                self.across(k, here).start()
+                self.outward(k, here).start()
+                self.swap(k).start()
+
+    def pass_on(self, ks, here):
+        for k in ks:
+            if self.first(k, here):
+                self.across(k, here).wait_recv()
+                self.outward(k, here).start()
+                self.swap(k).start()
+
+    def settle(self, here):
+        for k in range(len(self.x)):
+            self.across(k, here).wait_send()
+            self.outward(k, here).wait_send()
+            self.swap(k).wait()
+
+    def receive(self, here):
+        count = len(self.x)
+        for k in range(count):
+            self.copy(self.f[k], self.f[k], self.so.at[k], self.rr.at[k], self.z).wait_recv()
+            self.swap(k).start()
+        for k in range(count):
+            if k not in self.ready:
+                self.inward(k, here).wait_send()
+            self.swap(k).wait()
+
+    def greet(self, barrier, peers):
+        self.signal_all(barrier, peers)
+        self.wait_all(barrier, len(peers))
+
+    def signal_all(self, barrier, peers):
+        def signal(device):
+            pl.semaphore_signal(barrier, inc=1, device_id=device, device_id_type=pl.DeviceIdType.MESH)
+
+        for peer in peers + [(2 * self.z + 1 - self.core, self.me)]:
+            signal(peer)
+
+        @pl.when(self.z > 0)
+        def _():
+            signal((2 * self.z - 2 + self.core, self.me))
+
+        @pl.when(self.z < 3)
+        def _():
+            signal((2 * self.z + 2 + self.core, self.me))
+
+    def wait_all(self, barrier, peers):
+        pl.semaphore_wait(barrier, peers + 1 + jnp.minimum(self.z, 1) + jnp.minimum(3 - self.z, 1))
+
+
 def attn_sync_kernel(
-    qkv_ref, ot_ref, lse_ref, d0, d1, d2, d3, gst, w_ref, h0, h1, h2, h3,
+    qkv_hbm, ot_hbm, lse_ref, d0, d1, d2, d3, gst, w_hbm, h0, h1, h2, h3,
     nl, gd, ul_hbm, gu_hbm, m0, m1, m2, m3, gac, sums,
     a1_out, a2_out, b_out, g_out, qsums,
     ring, load_s, dot_, do_, kt, delta, dqt, dk, dv, dqkv, keep1, send1, got1, keep2, send2, got2,
-    bkeep, bsend, bgot, ra, rd, g0, g1, g2, g3, rg, core_s, core_r, wide_s, wide_r,
+    bkeep, bsend, bgot, ra, rd, g0, g1, g2, g3, rg, core_s, core_r, wide_s, wide_r, qkv_ref, ot_ref, w_ref, held,
+    xu, eu, z_s, z_r,
 ):
     n, me = lax.axis_index("narrow"), lax.axis_index("wide")
     core = n % 2
@@ -422,9 +535,11 @@
     MESH = pl.DeviceIdType.MESH
 
     barrier = pltpu.get_barrier_semaphore()
-    peers = [(n, xor2(me, r)) for r in range(1, 4)] + [(other, me)]
-    for peer in peers:
-        pl.semaphore_signal(barrier, inc=1, device_id=peer, device_id_type=MESH)
+    line = Line((n, me), *[[]] * 5, *[None] * 6)
+    line.signal_all(barrier, [(n, xor2(me, r)) for r in range(1, 4)])
+
+    def inward(here):
+        return line.copy(xu, eu, z_s, z_r, 1 if here in (0, 1) else 2)
 
     def load(i):
         if i < 4:
@@ -436,7 +551,16 @@
 
     load(0).start()
     load(1).start()
-    pl.semaphore_wait(barrier, 4)
+    late = [
+        pltpu.make_async_copy(src, dst, load_s.at[8 + i])
+        for i, (src, dst) in enumerate(
+            ((qkv_hbm, qkv_ref), (ot_hbm, ot_ref), (w_hbm, w_ref), (h0, held.at[0]), (h1, held.at[1]),
+             (h2, held.at[2]), (h3, held.at[3]))
+        )
+    ]
+    for c in late:
+        c.start()
+    line.wait_all(barrier, 3)
 
     def to_wide(i, r, src, dst):
         return pltpu.make_async_remote_copy(
@@ -465,28 +589,10 @@
         load(i + 2).start()
         if i == 1:
             core1.start()
-    extra = jnp.concatenate([sums[...], jnp.zeros((48, 768), f32)], axis=0).astype(bf16)
-    for j in range(4):
-        load(4 + j).wait()
-        down = tn(ring[j % 2], gd[...]).astype(bf16)
-        rel = xor2(me, j)
-        put(core == 0, keep2, send2, rel, 0, down[0:512])
-        put(core == 1, keep2, send2, rel, 0, down[512:768])
-        if j < 2:
-            load(6 + j).start()
-    for r, m in enumerate((m0, m1, m2, m3)):
-        put(core == 1, keep2, send2, r, 256, mm(m[...], gac[...]).astype(bf16))
-        put(core == 1, keep2, send2, r, 448, extra)
-    core2.start()
-    core1.wait()
-    for r in range(4):
-        keep1[r] = (keep1[r].astype(f32) + got1[r].astype(f32)).astype(bf16)
-    send_a = [to_wide(2 + r, r, keep1.at[r], ra.at[r - 1]) for r in (3, 1, 2)]
     for c in send_d:
         c.wait()
-    for c in send_a:
-        c.start()
-
+    for c in late:
+        c.wait()
     short = d0[:, FR : FR + 256].astype(f32)
     dot_[:, pl.ds(pl.multiple_of(FR * me, 128), FR)] = d0[:, 0:FR]
     for r in range(1, 4):
@@ -499,6 +605,13 @@
     for h in range(3):
         delta[h : h + 1, :] = jnp.sum(prod[64 * h : 64 * h + 64], axis=0, keepdims=True)
     kt[...] = qkv_ref[:, 256:448].astype(f32).T.astype(bf16)
+    core1.wait()
+    for r in range(4):
+        keep1[r] = (keep1[r].astype(f32) + got1[r].astype(f32)).astype(bf16)
+    send_a = [to_wide(2 + r, r, keep1.at[r], ra.at[r - 1]) for r in (3, 1, 2)]
+    for c in send_a:
+        c.start()
+
     keep_k, keep_v = [], []
     for h in range(3):
         cols = slice(64 * h, 64 * h + 64)
@@ -564,14 +677,36 @@
     first[2].start()
     project(2)
     first[3].start()
+    for c in send_a:
+        c.wait()
+    total = keep1[0].astype(f32) + ra[0].astype(f32) + ra[1].astype(f32) + ra[2].astype(f32)
+    xu[...] = total.astype(bf16)
+    line.at_ends(lambda here: inward(here).start())
     project(0)
     qsums[...] = jnp.sum(dqkv[...].astype(f32), axis=0, keepdims=True)
 
+    extra = jnp.concatenate([sums[...], jnp.zeros((16, 768), f32)], axis=0).astype(bf16)
+    for j in range(4):
+        load(4 + j).wait()
+        down = tn(ring[j % 2], gd[...]).astype(bf16)
+        rel = xor2(me, j)
+        put(core == 0, keep2, send2, rel, 0, down[0:496])
+        put(core == 1, keep2, send2, rel, 0, down[496:768])
+        if j < 2:
+            load(6 + j).start()
+    for r, m in enumerate((m0, m1, m2, m3)):
+        put(core == 1, keep2, send2, r, 272, mm(m[...], gac[...]).astype(bf16))
+        put(core == 1, keep2, send2, r, 464, extra)
+    core2.start()
+
     def join(part, half, i):
         part[:, half] = (part[:, half].astype(f32) + rg[i].astype(f32)).astype(bf16)
 
+    r_i, c_i = iota2((768, 640))
+    squeeze = ((r_i - 64 * (r_i >> 8) == c_i) & ((r_i & 255) < 192)).astype(f32).astype(bf16)
+
     def chunk_grad(chunk, r):
-        turned = chunk[...].astype(f32).T.astype(bf16)
+        turned = chunk.astype(f32).T.astype(bf16)
         value = (
             mm(turned[0:192, 0:384], dqkv[0:384, :])
             + mm(turned[192:384, 0:384], dqkv[384:768, :])
@@ -580,35 +715,42 @@
             + mm(turned[0:192, 768:864], dqkv[SLOTS : SLOTS + 96, :])
             + mm(turned[192:384, 768:864], dqkv[SLOTS + 96 : SLOTS + 192, :])
         ).astype(bf16)
+        value = mm(value, squeeze).astype(bf16)
         put(core == 0, bkeep, bsend, r, 0, value[0:96])
         put(core == 1, bkeep, bsend, r, 0, value[96:192])
 
-    chunk_grad(h0, 0)
-    chunk_grad(h1, 1)
-    for c in send_a:
-        c.wait()
-    a1_out[...] = (keep1[0].astype(f32) + ra[0].astype(f32) + ra[1].astype(f32) + ra[2].astype(f32)).astype(bf16)
     first[0].wait()
     join(g2, near, 0)
     second[0].start()
     first[1].wait()
     join(g1, far, 1)
     second[1].start()
-    chunk_grad(h2, 2)
-    chunk_grad(h3, 3)
+    for r in range(4):
+        chunk_grad(held[r], r)
     coreb.start()
     core2.wait()
     for r in range(4):
         a2_out[r] = (keep2[r].astype(f32) + got2[r].astype(f32)).astype(bf16)
-    first[2].wait()
-    first[3].wait()
     coreb.wait()
     for r in range(4):
         b_out[r] = (bkeep[r].astype(f32) + bgot[r].astype(f32)).astype(bf16)
+    first[2].wait()
+    first[3].wait()
     second[0].wait()
     g_out[:, near] = g0[:, near].astype(f32) + rg[2].astype(f32) + rg[4].astype(f32)
     second[1].wait()
     g_out[:, far] = g0[:, far].astype(f32) + rg[3].astype(f32) + rg[5].astype(f32)
+
+    def at_end(here):
+        inward(here).wait_send()
+        a1_out[...] = xu[...]
+
+    def at_middle(here):
+        inward(here).wait_recv()
+        a1_out[...] = (xu[...].astype(f32) + eu[...].astype(f32)).astype(bf16)
+
+    line.at_ends(at_end)
+    line.at_inner(at_middle)
 
 
 def attn_sync(qkv, ot, lse, dparts, gst, wqkv, first, nl, gd, ul, gu, mix, gac, sums):
@@ -618,15 +760,15 @@
     room = lambda *shape: pltpu.VMEM(shape, bf16)
     return pl.pallas_call(
         attn_sync_kernel,
-        in_specs=[vmem()] * 15 + [hbm] * 2 + [vmem()] * 6,
+        in_specs=[hbm] * 2 + [vmem()] * 6 + [hbm] * 5 + [vmem()] * 2 + [hbm] * 2 + [vmem()] * 6,
         out_specs=[vmem()] * 5,
         out_shape=[
-            sds((384, 768), bf16), sds((4, 512, 768), bf16), sds((4, 96, 768), bf16), sds((CH, TROWS), f32),
+            sds((384, 768), bf16), sds((4, 496, 768), bf16), sds((4, 96, 640), bf16), sds((CH, TROWS), f32),
             sds((1, 768), f32),
         ],
         scratch_shapes=[
             room(2, 768, 768),
-            sem((8,)),
+            sem((15,)),
             room(CH, TROWS),
             room(TROWS, CH),
             room(CH, TROWS),
@@ -637,18 +779,20 @@
             room(TROWS, 768),
         ]
         + [room(4, 384, 768)] * 3
-        + [room(4, 512, 768)] * 3
-        + [room(4, 96, 768)] * 3
+        + [room(4, 496, 768)] * 3
+        + [room(4, 96, 640)] * 3
         + [room(3, 384, 768), room(3, CH, 640)]
         + [room(CH, TROWS)] * 4
-        + [room(6, CH, 896), sem((3,)), sem((3,)), sem((12,)), sem((12,))],
+        + [room(6, CH, 896), sem((3,)), sem((3,)), sem((12,)), sem((12,))]
+        + [room(TROWS, 768), pltpu.VMEM((CH, TROWS), f32), room(768, 768), room(4, 864, 384)]
+        + [room(384, 768), room(384, 768), sem, sem],
         compiler_params=params(collective_id=2, has_side_effects=True),
         cost_estimate=cost(90),
         name="attn_sync",
     )(qkv, ot, lse, *dparts, gst, wqkv, *first, nl, gd, ul, gu, *mix, gac, sums)
 
 
-def wgrad_pair(pair, me, gsum, pre_ref, x_ref, sums_ref, half, gf, g_ref, gp, p0, p1, bb, g2, xt):
+def wgrad_front(pair, gsum, pre_ref, sums_ref, half, gf, g_ref, gp):
     at = pl.ds(pl.multiple_of(96 * pair, 32), 96)
     total = gsum[at, :]
     pad = jnp.zeros((16, TROWS), f32)
@@ -670,88 +814,48 @@
     extra = jnp.concatenate(
         [sums_ref[...], jnp.concatenate([bias_sum, jnp.zeros((1, 640), f32)], axis=1), jnp.zeros((14, 768), f32)], axis=0
     )
-    for r in range(4):
-        half[r, 192:208, :] = extra.astype(bf16)
-
+    half[0, 192:208, :] = extra.astype(bf16)
+
+
+def wgrad_group(pair, j, me, x_ref, half, gp, p0, bb, g2, xt):
     lane = lax.broadcasted_iota(jnp.int32, (TROWS, 128), 1)
     here, before = gp[16 : 16 + TROWS, :], gp[15 : 15 + TROWS, :]
-    a, b = pair_slots(x_ref.at[pair], 1920)
-    p0[...] = a
-    p1[...] = b
+    p0[...] = pair_slots(x_ref.at[pair], 1920, (j,))[0]
     pack0, pack1 = gather_slots((256, 384), 0), gather_slots((256, 384), 192)
-    for j in range(2):
-        bb[0:16, :] = jnp.zeros((16, 128), f32)
-        if j == 0:
-            bb[16 : 16 + TROWS, :] = jnp.where(lane < 64, here, pltpu.roll(before, 64, 1))
-        else:
-            bb[16 : 16 + TROWS, :] = jnp.where(lane < 64, pltpu.roll(here, 64, 1), before)
-        for p in range(8):
-            g2[:, 128 * p : 128 * p + 128] = bb[16 - 2 * p : 16 - 2 * p + TROWS, :].astype(bf16)
-        slots = (p0, p1)[j]
-        for q in range(4):
-            xt[128 * q : 128 * q + 128, :] = slots[32 * q : 32 * q + TROWS, :].astype(f32).T.astype(bf16)
-        for side in range(2):
-            base = 512 * side
-            left = mm(xt[...], g2[:, base : base + 256]).astype(bf16)
-            right = mm(xt[...], g2[:, base + 256 : base + 512]).astype(bf16)
-            packed = (mm(left, pack0) + mm(right, pack1)).astype(bf16)
-            for m in range(4):
-                tile = jnp.concatenate([packed[128 * m : 128 * m + 48], packed[128 * m + 64 : 128 * m + 112]], axis=0)
-                half[xor2(me, m), 96 * j : 96 * j + 96, 384 * side : 384 * side + 384] = tile
+    bb[0:16, :] = jnp.zeros((16, 128), f32)
+    if j == 0:
+        bb[16 : 16 + TROWS, :] = jnp.where(lane < 64, here, pltpu.roll(before, 64, 1))
+    else:
+        bb[16 : 16 + TROWS, :] = jnp.where(lane < 64, pltpu.roll(here, 64, 1), before)
+    for p in range(8):
+        g2[:, 128 * p : 128 * p + 128] = bb[16 - 2 * p : 16 - 2 * p + TROWS, :].astype(bf16)
+    for q in range(4):
+        xt[128 * q : 128 * q + 128, :] = p0[32 * q : 32 * q + TROWS, :].astype(f32).T.astype(bf16)
+    for side in range(2):
+        base = 512 * side
+        left = mm(xt[...], g2[:, base : base + 256]).astype(bf16)
+        right = mm(xt[...], g2[:, base + 256 : base + 512]).astype(bf16)
+        packed = (mm(left, pack0) + mm(right, pack1)).astype(bf16)
+        for m in range(4):
+            tile = jnp.concatenate([packed[128 * m : 128 * m + 48], packed[128 * m + 64 : 128 * m + 112]], axis=0)
+            half[xor2(me, m), 96 * j : 96 * j + 96, 384 * side : 384 * side + 384] = tile
 
 
 def conv_sync_kernel(
-    gsum, pre_ref, x_ref, sums_ref, wd_ref, xu, a_ref, b_ref,
+    gsum, pre_ref, x_ref, sums_ref, xu, wd_hbm, a_hbm, b_ref,
     fu, fa, fb, fc, ou, oa, ob, oc, f0, f1, f2, f3,
     gp, p0, p1, bb, g2, xt, y_ref, t_ref, gf, g, fg, s1, s2, s3,
-    csend, ckeep, cgot, ra, rb, rc, xa, xb, eu, ea, eb, ec, yu, ya, yb, yc,
-    ss, so, re, rr, sc, rcv, wide_s, wide_r, core_s, core_r,
+    csend, ckeep, cgot, ra, rb, rc, xa, xb, eu, ea, eb, ec, yu, ya, yb, yc, next1, next2,
+    z0, z1, z2, z3, z4, z5, wide_s, wide_r, core_s, core_r, wd_ref, load_s,
 ):
     n, me = lax.axis_index("narrow"), lax.axis_index("wide")
-    z, core = n // 2, n % 2
-    MESH = pl.DeviceIdType.MESH
-
-    def copy(src, dst, send, recv, device):
-        return pltpu.make_async_remote_copy(
-            src_ref=src, dst_ref=dst, send_sem=send, recv_sem=recv, device_id=device, device_id_type=MESH
-        )
-
-    def along(zz, cc=core):
-        return (2 * zz + cc, me)
-
-    barrier = pltpu.get_barrier_semaphore()
-
-    def greet(device):
-        pl.semaphore_signal(barrier, inc=1, device_id=device, device_id_type=MESH)
-
-    for r in range(1, 4):
-        greet((n, xor2(me, r)))
-    greet(along(z, 1 - core))
-
-    @pl.when(z > 0)
-    def _():
-        greet(along(z - 1))
-
-    @pl.when(z < 3)
-    def _():
-        greet(along(z + 1))
-
-    pl.semaphore_wait(barrier, 4 + jnp.minimum(z, 1) + jnp.minimum(3 - z, 1))
-
-    def over_wide(which, r, src, dst):
-        return copy(src, dst, wide_s.at[3 * which + r - 1], wide_r.at[3 * which + r - 1], (n, xor2(me, r)))
-
-    send_b = [over_wide(0, r, b_ref.at[r], rb.at[r - 1]) for r in (3, 1, 2)]
-    send_a = [over_wide(1, r, a_ref.at[r], ra.at[r - 1]) for r in (3, 1, 2)]
-    for c in send_b + send_a:
-        c.start()
+    core = n % 2
 
     pieces = [(3, None, 96 * r, 96) for r in range(4)]
-    pieces += [(0, r, 0, 96) for r in range(4)] + [(1, None, 128 * r, 128) for r in range(4)]
-    for r in range(4):
-        pieces += [(2, r, 0, 112), (2, r, 112, 96)]
-    count = len(pieces)
-    set_u, set_b, set_a, set_c = range(0, 4), range(4, 8), range(8, 12), range(12, count)
+    pieces += [(0, r, 0, 96) for r in range(4)] + [(2, r, 0, 96) for r in range(4)]
+    pieces += [(1, None, 0, 128), (1, None, 128, 128), (1, None, 256, 128), (1, None, 384, 112)]
+    pieces += [(2, 0, 96, 112), (2, 1, 96, 96), (2, 2, 96, 48), (2, 2, 144, 48), (2, 3, 96, 48), (2, 3, 144, 48)]
+    set_u, set_b, set_c, set_a, set_d = range(0, 4), range(4, 8), range(8, 12), range(12, 16), range(16, 22)
 
     def views(refs):
         out = []
@@ -760,67 +864,60 @@
             out.append(ref.at[row : row + rows] if r is None else ref.at[r, row : row + rows])
         return out
 
-    x, e, y, f, o = (views(refs) for refs in ((xb, xa, csend, xu), (eb, ea, ec, eu), (yb, ya, yc, yu), (fb, fa, fc, fu), (ob, oa, oc, ou)))
-
-    def first(k, here):
-        return k % 2 == (0 if here == 1 else 1)
-
-    def swap(k):
-        return copy(f[k], o[k], sc.at[k], rcv.at[k], along(z, 1 - core))
-
-    def inward(k, here):
-        return copy(x[k], e[k], ss.at[k], re.at[k], along(1 if here == 0 else 2))
-
-    def across(k, here):
-        src = y[k] if first(k, here) else f[k]
-        return copy(src, src, ss.at[k], rr.at[k], along(3 - here))
-
-    def outward(k, here):
-        return copy(f[k], f[k], so.at[k], rr.at[k], along(0 if here == 1 else 3))
-
-    def at_ends(do):
-        pl.when(z == 0)(lambda: do(0))
-        pl.when(z == 3)(lambda: do(3))
-
-    def at_inner(do):
-        pl.when(z == 1)(lambda: do(1))
-        pl.when(z == 2)(lambda: do(2))
-
-    def begin(ks):
-        def do(here):
-            for k in ks:
-                inward(k, here).start()
-
-        at_ends(do)
-
-    def meet(ks, here):
-        for k in ks:
-            inward(k, here).wait_recv()
-            if first(k, here):
-                y[k][...] = (x[k][...].astype(f32) + e[k][...].astype(f32)).astype(bf16)
-                across(k, here).start()
-
-    def close(ks, here):
-        for k in ks:
-            if not first(k, here):
-                across(k, here).wait_recv()
-                f[k][...] = (x[k][...].astype(f32) + e[k][...].astype(f32) + y[k][...].astype(f32)).astype(bf16)
-                across(k, here).start()
-                outward(k, here).start()
-                swap(k).start()
-
-    def pass_on(ks, here):
-        for k in ks:
-            if first(k, here):
-                across(k, here).wait_recv()
-                outward(k, here).start()
-                swap(k).start()
-
-    def wgrad(pair, half, slot):
-        wgrad_pair(
-            pair, me, gsum, pre_ref, x_ref, sums_ref, half, gf.at[slot], g.at[slot],
-            gp, p0, p1, bb, g2, xt,
+    sets = ((xb, xa, csend, xu), (eb, ea, ec, eu), (yb, ya, yc, yu), (fb, fa, fc, fu), (ob, oa, oc, ou))
+    line = Line((n, me), *(views(refs) for refs in sets), z0, z1, z2, z3, z4, z5, set_u)
+    loads = [
+        pltpu.make_async_copy(wd_hbm, wd_ref, load_s.at[0]),
+        pltpu.make_async_copy(a_hbm.at[0], xa, load_s.at[1]),
+        pltpu.make_async_copy(a_hbm.at[2, 0:256], next1, load_s.at[2]),
+        pltpu.make_async_copy(a_hbm.at[1, 256:496], next2, load_s.at[3]),
+    ]
+    for c in loads:
+        c.start()
+    line.greet(pltpu.get_barrier_semaphore(), [(n, xor2(me, r)) for r in range(1, 4)])
+
+    def to_wide(sem, r, src, dst):
+        return pltpu.make_async_remote_copy(
+            src_ref=src, dst_ref=dst, send_sem=wide_s.at[sem], recv_sem=wide_r.at[sem],
+            device_id=(n, xor2(me, r)), device_id_type=pl.DeviceIdType.MESH,
         )
+
+    def over_wide(which, src, dst):
+        return [to_wide(3 * which + r - 1, r, src(r), dst(r)) for r in (3, 1, 2)]
+
+    def start(copies):
+        for c in copies:
+            c.start()
+
+    def wait(copies):
+        for c in copies:
+            c.wait()
+
+    halves = (slice(0, 256), slice(256, 496))
+    send_b = over_wide(0, lambda r: b_ref.at[r], lambda r: rb.at[r - 1])
+    near, far = halves
+    send_a = [
+        to_wide(3, 1, a_hbm.at[3, near], ra.at[0, near]), to_wide(4, 2, a_hbm.at[3, far], ra.at[0, far]),
+        to_wide(5, 1, a_hbm.at[1, near], ra.at[1, near]), to_wide(6, 2, a_hbm.at[2, far], ra.at[1, far]),
+        to_wide(7, 2, next1, ra.at[2, near]), to_wide(8, 1, next2, ra.at[2, far]),
+    ]
+    groups = (slice(0, 96), slice(96, 192))
+    send_c = [
+        over_wide(3 + i, lambda r, at=at: ckeep.at[r, at], lambda r, at=at: rc.at[r - 1, at])
+        for i, at in enumerate(groups)
+    ]
+    send_f = over_wide(5, lambda r: (s1, s2, s3)[r - 1], lambda r: (f1, f2, f3)[r - 1])
+    crossing = (slice(0, 96), slice(96, 208))
+    to_core = [
+        line.copy(csend.at[:, at], cgot.at[:, at], core_s.at[i], core_r.at[i], line.z, 1 - core)
+        for i, at in enumerate(crossing)
+    ]
+    start(send_b)
+    start(send_a[:4])
+    line.at_inner(lambda here: line.meet(set_u, here))
+
+    def group(pair, j, half, slot):
+        wgrad_group(pair, j, me, x_ref, half, gp.at[slot], p0, bb, g2, xt)
 
     def dgrad(pair, slot):
         a, b = pair_slots(g.at[slot], 1920)
@@ -829,43 +926,67 @@
         value = conv_block((p0, p1), wd_ref.at[pl.ds(2 * pair, 2)], y_ref, t_ref, 1) + gf[slot]
         fg[pair] = value.astype(bf16)
 
-    begin(set_u)
-    wgrad(1 - core, csend, 0)
-    to_core = copy(csend, cgot, core_s, core_r, along(z, 1 - core))
-    to_core.start()
-    for c in send_b:
-        c.wait()
+    def add_a(i):
+        wait([send_a[2 + i], send_a[4 + i]])
+        at = halves[i]
+        xa[at] = (xa[at].astype(f32) + ra[1, at].astype(f32) + ra[2, at].astype(f32)).astype(bf16)
+        line.begin(set_a[2 * i : 2 * i + 2])
+
+    def add_core(i):
+        to_core[i].wait()
+        at = crossing[i]
+        for r in range(4):
+            ckeep[r, at] = (ckeep[r, at].astype(f32) + cgot[r, at].astype(f32)).astype(bf16)
+        start(send_c[i])
+
+    def take_c(i):
+        wait(send_c[i])
+        csend[0, crossing[i]] = ckeep[0, crossing[i]]
+        for r in range(1, 4):
+            csend[r, groups[i]] = rc[r - 1, groups[i]]
+        line.begin((set_c, set_d)[i])
+
+    def inner(*does):
+        def do(here):
+            for act, ks in does:
+                act(ks, here)
+
+        line.at_inner(do)
+
+    meet, close, pass_on = line.meet, line.close, line.pass_on
+    wgrad_front(1 - core, gsum, pre_ref, sums_ref, csend, gf.at[0], g.at[0], gp.at[0])
+    group(1 - core, 0, csend, 0)
+    to_core[0].start()
+    inner((close, set_u))
+    wait(send_b)
     xb[0] = b_ref[0]
     for r in range(1, 4):
         xb[r] = rb[r - 1]
-    begin(set_b)
-    at_inner(lambda here: meet(set_u, here))
-
-    wgrad(core, ckeep, 1)
-    to_core.wait()
-    for r in range(4):
-        ckeep[r] = (ckeep[r].astype(f32) + cgot[r].astype(f32)).astype(bf16)
-    send_c = [over_wide(2, r, ckeep.at[r], rc.at[r - 1]) for r in (3, 1, 2)]
-    for c in send_c:
-        c.start()
-
-    def inner_b(here):
-        close(set_u, here)
-        meet(set_b, here)
-
-    at_inner(inner_b)
+    line.begin(set_b)
+    wgrad_front(core, gsum, pre_ref, sums_ref, ckeep, gf.at[1], g.at[1], gp.at[1])
+    group(core, 0, ckeep, 1)
+    inner((pass_on, set_u), (meet, set_b[0:2]))
+    add_core(0)
+    group(1 - core, 1, csend, 0)
+    to_core[1].start()
+    inner((meet, set_b[2:4]), (close, set_b[0:2]))
+    wait(loads)
+    wait(send_a[0:2])
+    next1[...] = (next1[...].astype(f32) + ra[0, near].astype(f32)).astype(bf16)
+    next2[...] = (next2[...].astype(f32) + ra[0, far].astype(f32)).astype(bf16)
+    start(send_a[4:6])
+    take_c(0)
+    group(core, 1, ckeep, 1)
+    inner((close, set_b[2:4]), (pass_on, set_b[0:2]))
+    add_core(1)
+    inner((meet, set_c[0:2]))
+    add_a(0)
     dgrad(1 - core, 0)
-
-    def inner_c(here):
-        pass_on(set_u, here)
-        close(set_b, here)
-
-    at_inner(inner_c)
-    for c in send_a:
-        c.wait()
-    xa[...] = (a_ref[0].astype(f32) + ra[0].astype(f32) + ra[1].astype(f32) + ra[2].astype(f32)).astype(bf16)
-    begin(set_a)
+    inner((pass_on, set_b[2:4]), (close, set_c[0:2]), (meet, set_c[2:4]))
+    add_a(1)
+    take_c(1)
     dgrad(core, 1)
+    inner((pass_on, set_c[0:2]), (meet, set_a[0:2]), (close, set_c[2:4]))
     pack0, pack1 = gather_slots((256, 384), 0), gather_slots((256, 384), 192)
 
     def rows_of(lo, rows):
@@ -881,78 +1002,55 @@
             def _():
                 outs[r][...] = chunk
 
-    for c in send_c:
-        c.wait()
-    csend[0] = ckeep[0]
-    for r in range(1, 4):
-        csend[r] = rc[r - 1]
-    begin(set_c)
-    send_f = [over_wide(3, r, (s1, s2, s3)[r - 1], (f1, f2, f3)[r - 1]) for r in (3, 1, 2)]
-    for c in send_f:
-        c.start()
-
-    def inner(here):
-        pass_on(set_b, here)
-        rest = list(set_a) + list(set_c)
-        for i in range(0, len(rest), 2):
-            pair = rest[i : i + 2]
-            meet(pair, here)
-            close(pair, here)
-            if i:
-                pass_on(rest[i - 2 : i], here)
-        pass_on(rest[-2:], here)
-        for k in range(count):
-            across(k, here).wait_send()
-            outward(k, here).wait_send()
-            swap(k).wait()
-
-    def outer(here):
-        for k in range(count):
-            copy(f[k], f[k], so.at[k], rr.at[k], along(z)).wait_recv()
-            swap(k).start()
-        for k in range(count):
-            inward(k, here).wait_send()
-            swap(k).wait()
-
-    at_inner(inner)
-    at_ends(outer)
-    for c in send_f:
-        c.wait()
-
-
-def conv_sync(gsum, pre, xp, sums, wd, up_sum, ffn_halves, qkv_halves):
+    start(send_f)
+
+    rest = [set_a[0:2], set_a[2:4], set_d[0:2], set_d[2:4], set_d[4:6]]
+    does = []
+    for i, pair in enumerate(rest):
+        if i + 1 < len(rest):
+            does.append((meet, rest[i + 1]))
+        does.append((close, pair))
+        does.append((pass_on, rest[i - 1] if i else set_c[2:4]))
+    inner(*does, (pass_on, rest[-1]), (lambda ks, here: line.settle(here), None))
+    line.at_ends(line.receive)
+    wait(send_f)
+
+
+def conv_sync(gsum, pre, xp, sums, up_sum, wd, ffn_halves, qkv_halves):
     sds = jax.ShapeDtypeStruct
-    shapes = [(384, 768), (512, 768), (4, 96, 768), (4, 208, 768)]
+    shapes = [(384, 768), (496, 768), (4, 96, 640), (4, 208, 768)]
+    hbm = pl.BlockSpec(memory_space=pl.ANY)
     sem = pltpu.SemaphoreType.DMA
+    room = lambda *shape: pltpu.VMEM(shape, bf16)
     return pl.pallas_call(
         conv_sync_kernel,
-        in_specs=[vmem()] * 8,
+        in_specs=[vmem()] * 5 + [hbm] * 2 + [vmem()],
         out_specs=[vmem()] * 12,
         out_shape=[sds(v, bf16) for v in shapes * 2] + [sds((256, 384), bf16)] * 4,
         scratch_shapes=[
+            pltpu.VMEM((2, 16 + TROWS, 128), f32),
+            room(1920, 128),
+            room(1920, 128),
             pltpu.VMEM((16 + TROWS, 128), f32),
-            pltpu.VMEM((1920, 128), bf16),
-            pltpu.VMEM((1920, 128), bf16),
-            pltpu.VMEM((16 + TROWS, 128), f32),
-            pltpu.VMEM((TROWS, 1024), bf16),
-            pltpu.VMEM((512, TROWS), bf16),
+            room(TROWS, 1024),
+            room(512, TROWS),
             pltpu.VMEM((CB + 16, 1024), f32),
             pltpu.VMEM((CB + 8, 128), f32),
             pltpu.VMEM((2, TROWS, 128), f32),
-            pltpu.VMEM((2, 1936, 128), bf16),
-            pltpu.VMEM((2, TROWS, 128), bf16),
+            room(2, 1936, 128),
+            room(2, TROWS, 128),
         ]
-        + [pltpu.VMEM((256, 384), bf16)] * 3
-        + [pltpu.VMEM((4, 208, 768), bf16)] * 3
-        + [pltpu.VMEM((3, 512, 768), bf16), pltpu.VMEM((3, 96, 768), bf16), pltpu.VMEM((3, 208, 768), bf16)]
-        + [pltpu.VMEM((512, 768), bf16), pltpu.VMEM((4, 96, 768), bf16)]
-        + [pltpu.VMEM(v, bf16) for v in shapes * 2]
-        + [sem((20,))] * 6
-        + [sem((12,)), sem((12,)), sem, sem],
+        + [room(256, 384)] * 3
+        + [room(4, 208, 768)] * 3
+        + [room(3, 496, 768), room(3, 96, 640), room(3, 192, 768), room(496, 768), room(4, 96, 640)]
+        + [room(*v) for v in shapes * 2]
+        + [room(256, 768), room(240, 768)]
+        + [sem((22,))] * 6
+        + [sem((18,)), sem((18,)), sem((2,)), sem((2,)), room(4, 512, 1024), sem((4,))],
         compiler_params=params(collective_id=1, has_side_effects=True),
         cost_estimate=cost(100),
         name="conv_sync",
-    )(gsum, pre, xp, sums, wd, up_sum, ffn_halves, qkv_halves)
+    )(gsum, pre, xp, sums, up_sum, wd, ffn_halves, qkv_halves)
 
 
 def unpack_frames_kernel(s_ref, c0, c1, c2, c3, o_ref):
@@ -1170,18 +1268,18 @@
     for j in range(4):
         row = 192 * (j & 1)
         up[:, 768 * j : 768 * j + 768] = a1[j >> 1, row : row + 192, :].astype(f32)
-    down[0:512, :] = a2[0].astype(f32)
-    down[512:768, :] = a2[1, 0:256, :].astype(f32)
-    out[...] = a2[1, 256:448, :].astype(f32)
-    small[...] = a2[1, 448:464, :].astype(f32)
+    down[0:496, :] = a2[0].astype(f32)
+    down[496:768, :] = a2[1, 0:272, :].astype(f32)
+    out[...] = a2[1, 272:464, :].astype(f32)
+    small[...] = a2[1, 464:480, :].astype(f32)
     r_i, c_i = iota2((256, 768))
     totals = [jnp.zeros((CH, 768), f32)] * 3
     for r in range(4):
         base = 192 * (me ^ r)
-        hit = (c_i - base == r_i) & (r_i < 192)
-        move = hit.astype(f32).astype(bf16)
-        for k in range(3):
-            totals[k] = totals[k] + mm(b_ref[r, :, 256 * k : 256 * k + 256], move)
+        inside = (c_i >= base) & (c_i < base + 192)
+        at0, at64 = (((c_i - base == r_i - skip) & inside).astype(f32).astype(bf16) for skip in (0, 64))
+        for k, (lane0, move) in enumerate(((0, at0), (128, at64), (384, at0))):
+            totals[k] = totals[k] + mm(b_ref[r, :, lane0 : lane0 + 256], move)
     wq[...], wk[...], wv[...] = totals
 
 
@@ -1194,8 +1292,8 @@
         out_shape=[sds((CH, 3072), f32), sds((768, 768), f32)] + [sds((CH, 768), f32)] * 4 + [sds((16, 768), f32)],
         scratch_shapes=[
             pltpu.VMEM((2, 384, 768), bf16),
-            pltpu.VMEM((2, 512, 768), bf16),
-            pltpu.VMEM((4, CH, 768), bf16),
+            pltpu.VMEM((2, 496, 768), bf16),
+            pltpu.VMEM((4, CH, 640), bf16),
         ],
         compiler_params=params(),
         cost_estimate=cost(6),
@@ -1228,7 +1326,7 @@
         qkv, mixed_t, lse, [x0, x1, x2, x3], gst, wqkv, first, nl, gd, ul, gu, mix, gac, sums
     )
     own1, own2, ownb, ownc, other1, other2, otherb, otherc, *fchunks = conv_sync(
-        gsum, pre, xp, qkv_sums, wd, up_sum, ffn_halves, qkv_halves
+        gsum, pre, xp, qkv_sums, up_sum, wd, ffn_halves, qkv_halves
     )
     frames_grad = unpack_frames(scal, fchunks)
     up, down, out, wq, wk, wv, small = finish(scal, own1, other1, own2, other2, ownb, otherb)

time: 333 us -> 311 us (0.934)
  Pallas kernels: 316 us -> 294 us
    pallas_call x2, Pallas kernels: 197 us -> 174 us  [the longest x1 105 us: conv_sync(): pl.pallas_call(conv_sync_kernel, in_specs=[vmem()] * 5 + [hbm] * 2 + [vme...]
where the time goes in v1:
time: 311 us; the launch traced here: 307 us
  Pallas kernels  294 us (95%)
  local copies, waits for them, and re-layouts  7.78 us (3%)
  other arithmetic  3.3 us (1%)
    pallas_call x1, Pallas kernels, conv_sync(): pl.pallas_call(conv_sync_kernel, in_specs=[vmem()] * 5 + [hbm] * 2 + [vme...  105 us
    pallas_call x1, Pallas kernels, front_sync(): pl.pallas_call(front_sync_kernel, in_specs=[vmem()] * 4 + [pl.BlockSpec(m...  70.5 us
    pallas_call x1, Pallas kernels, attn_sync(): pl.pallas_call(attn_sync_kernel, in_specs=[hbm] * 2 + [vmem()] * 6 + [hbm...  69.2 us
    pallas_call x1, Pallas kernels, ffn(): pl.pallas_call(ffn_kernel, in_specs=[smem()] + [vmem()] * 6 + [hbm, vmem(...  28.8 us
    pallas_call x1, Pallas kernels, kernel_out(): pl.pallas_call(kernel_out_kernel, grid_spec=pltpu.PrefetchScalarGridSpec(...  7.7 us

profile of v1, /device:TPU:0, one launch (start us, length us, event | category | flops | bytes accessed | tf_op | source)
XLA Modules:
  0.0 307.3 jit_solution(8834052753649439176)
XLA Ops:
  0.7 1.3 fusion.2
  3.3 0.6 pad_add_fusion.s_ref
  3.9 0.0 copy-start.1
  3.9 0.0 copy-start.2
  3.9 0.0 copy-start.3
  3.9 3.4 %pack_frames.1 = (bf16[256,384]{1,0:T(8,128)(2,1)}, bf16[256,384]{1,0:T(8,128)(2,1)}, bf16[256,384]{1,0:T(8,128)(2,1)}, bf16[256,384]{1,0:T(8,128)(2,1)}) custom-call(s32[4]{0:T(128)} %pad_add_fusion.s_ref, bf16[2,384,768]{2,1,0:T(8,128)(2,1)} %x_ref.1), custom_call_target="tpu_custom_call" | custom-call | flops 3000000000 | bytes 10200000 | tf_op jit(solution)/shard_map/pack_frames/pallas_call | solution.py:131
  7.3 0.0 copy-done.1
  7.3 0.0 copy-done.2
  7.3 0.0 copy-done.3
  7.4 0.1 pad.5.clone
  7.5 0.7 maximum_maximum_fusion.vec
  8.1 0.0 copy-start
  8.1 0.0 copy-start.4
  8.1 0.0 copy-start.5
  8.2 0.0 copy-start.6
  8.2 0.0 copy-start.7
  8.2 0.0 copy-start.8
  8.2 0.0 copy-start.9
  8.2 70.5 %front_sync.1 = (bf16[4,512,1024]{2,1,0:T(8,128)(2,1)}, f32[2,1792,128]{2,1,0:T(8,128)}, bf16[2,1936,128]{2,1,0:T(8,128)(2,1)}, bf16[864,384]{1,0:T(8,128)(2,1)}...) custom-call(bf16[256,384]{1,0:T(8,128)(2,1)} %get-tuple-element.77.p, ...), custom_call_target="tpu_custom_call" | custom-call | flops 65000001536 | bytes 221000000 | tf_op jit(solution)/shard_map/front_sync/pallas_call | solution.py:381
  78.7 0.0 copy-done
  78.7 0.6 broadcast_in_dim.11
  79.3 0.0 copy-done.4
  79.3 0.0 copy-done.5
  79.3 0.0 copy-done.6
  79.3 0.0 copy-done.7
  79.3 0.0 copy-done.8
  79.4 0.0 copy-done.9
  79.4 0.6 convert_element_type.7.vecs
  80.0 28.8 %ffn.1 = (bf16[2,384,768]{2,1,0:T(8,128)(2,1)}, bf16[768,3072]{1,0:T(8,128)(2,1)}, bf16[768,3072]{1,0:T(8,128)(2,1)}, bf16[768,768]{1,0:T(8,128)(2,1)}, bf16[768...) custom-call(s32[4]{0:T(128)} %pad_add_fusion.s_ref, ...), custom_call_target="tpu_custom_call" | custom-call | flops 28000000000 | bytes 95200000 | tf_op jit(solution)/shard_map/ffn/pallas_call | solution.py:1230
  108.8 69.2 %attn_sync.1 = (bf16[384,768]{1,0:T(8,128)(2,1)}, bf16[4,496,768]{2,1,0:T(8,128)(2,1)}, bf16[4,96,640]{2,1,0:T(8,128)(2,1)}, f32[192,1792]{1,0:T(8,128)}, f32[1,768]{1,0:T(1,128)}) custom-call(bf16[1792,768]{1,0:T(8,128)(2,1)} %get-tuple-element.87.qkv_hbm, f32[192,1792]{1,0:T(8,128)} %get-tuple-element.88.ot_hbm, f32[8,1792]{1,0:T(8,128)} %get-tuple-element.89.lse_ref, ...), custom_call_target="tpu_custom_call" | custom-call | flops 89999998976 | bytes 306000000 | tf_op jit(solution)/shard_map/attn_sync/pallas_call | solution.py:761
  178.1 104.7 %conv_sync.1 = (bf16[384,768]{1,0:T(8,128)(2,1)}, bf16[496,768]{1,0:T(8,128)(2,1)}, bf16[4,96,640]{2,1,0:T(8,128)(2,1)}, bf16[4,208,768]{2,1,0:T(8,128)(2,1)}, b...) custom-call(f32[192,1792]{1,0:T(8,128)} %get-tuple-element.106.gsum,, ...), custom_call_target="tpu_custom_call" | custom-call | flops 99999997952 | bytes 340000000 | tf_op jit(solution)/shard_map/conv_sync/pallas_call | solution.py:1025
  282.7 3.2 %unpack_frames.1 = bf16[2,384,768]{2,1,0:T(8,128)(2,1)} custom-call(s32[4]{0:T(128)} %pad_add_fusion.s_ref, bf16[256,384]{1,0:T(8,128)(2,1)} %get-tuple-element.114.c0, bf16[256,384]{1,0:T(8,128)(2,1)} %get-tuple-element.115.c1, bf16[256,384]{1,0:T(8,128)(2,1)} %get-tuple-element.116.c2, bf16[256,384]{1,0:T(8,128)(2,1)} %get-tuple-element.117.c3), custom_call_target="tpu_custom_call" | custom-call | flops 3000000000 | bytes 10200000 | tf_op jit(solution)/shard_map/unpack_frames/pallas_call | solution.py:1074
  286.0 7.7 %kernel_grad_out.1 = (f32[32,16,48,48]{3,2,1,0:T(8,128)}, bf16[2,16,768]{2,1,0:T(8,128)(2,1)}) custom-call(s32[4]{0:T(128)} %pad_add_fusion.s_ref, bf16[4,208,768]{2,1,0:T(8,128)(2,1)} %get-tuple-element.118.own_ref, bf16[4,208,768]{2,1,0:T(8,128)(2,1)} %get-tuple-element.119.other_ref), custom_call_target="tpu_custom_call" | custom-call | flops 8999999488 | bytes 30600000 | tf_op jit(solution)/shard_map/kernel_grad_out/pallas_call | solution.py:1101
  293.7 0.8 convert_element_type.8
  294.5 0.1 concatenate.13
  294.6 0.1 concatenate.12
  294.7 0.6 reshape.57
  295.3 6.1 %weight_grads_out.1 = (f32[192,3072]{1,0:T(8,128)}, f32[768,768]{1,0:T(8,128)}, f32[192,768]{1,0:T(8,128)}, f32[192,768]{1,0:T(8,128)}, f32[192,768]{1,0:T(8,128...) custom-call(s32[4]{0:T(128)} %pad_add_fusion.s_ref, bf16[384,768]{1,0:T(8,128)(2,1)} %get-tuple-element.122.own1, ...), custom_call_target="tpu_custom_call" | custom-call | flops 6000000000 | bytes 20400000 | tf_op jit(solution)/shard_map/weight_grads_out/pallas_call | solution.py:1288
  301.4 1.3 fusion.1
  302.7 0.9 fusion
  303.6 0.6 constant_dynamic-slice_fusion.4
  304.2 0.6 constant_dynamic-slice_fusion.2
  304.9 0.7 slice.52
  305.6 0.6 dynamic-slice_reduce_fusion
  306.2 0.6 constant_dynamic-slice_fusion
  (13 shorter events, 0.1 us)
Async XLA Ops:
  3.9 3.4 %copy-start.1 = (bf16[768]{0:T(1024)(128)(2,1)S(1)}, bf16[768]{0:T(1024)(128)(2,1)}, u32[]{:S(2)}) copy-start(bf16[768]{0:T(1024)(128)(2,1)} %param.28) | copy-start | bytes 4612
  3.9 3.5 %copy-start.2 = (bf16[768]{0:T(1024)(128)(2,1)S(1)}, bf16[768]{0:T(1024)(128)(2,1)}, u32[]{:S(2)}) copy-start(bf16[768]{0:T(1024)(128)(2,1)} %param.25) | copy-start | bytes 4612
  3.9 3.5 %copy-start.3 = (bf16[768]{0:T(1024)(128)(2,1)S(1)}, bf16[768]{0:T(1024)(128)(2,1)}, u32[]{:S(2)}) copy-start(bf16[768]{0:T(1024)(128)(2,1)} %param.23) | copy-start | bytes 4612
  8.1 70.5 %copy-start = (bf16[3072]{0:T(1024)(128)(2,1)S(1)}, bf16[3072]{0:T(1024)(128)(2,1)}, u32[]{:S(2)}) copy-start(bf16[3072]{0:T(1024)(128)(2,1)} %param.34) | copy-start | bytes 18436
  8.1 71.1 %copy-start.4 = (bf16[768]{0:T(1024)(128)(2,1)S(1)}, bf16[768]{0:T(1024)(128)(2,1)}, u32[]{:S(2)}) copy-start(bf16[768]{0:T(1024)(128)(2,1)} %param.30) | copy-start | bytes 4612
  8.1 71.1 %copy-start.5 = (bf16[768]{0:T(1024)(128)(2,1)S(1)}, bf16[768]{0:T(1024)(128)(2,1)}, u32[]{:S(2)}) copy-start(bf16[768]{0:T(1024)(128)(2,1)} %param.31) | copy-start | bytes 4612
  8.2 71.1 %copy-start.6 = (bf16[768]{0:T(1024)(128)(2,1)S(1)}, bf16[768]{0:T(1024)(128)(2,1)}, u32[]{:S(2)}) copy-start(bf16[768]{0:T(1024)(128)(2,1)} %param.32) | copy-start | bytes 4612
  8.2 71.2 %copy-start.7 = (bf16[768]{0:T(1024)(128)(2,1)S(1)}, bf16[768]{0:T(1024)(128)(2,1)}, u32[]{:S(2)}) copy-start(bf16[768]{0:T(1024)(128)(2,1)} %param.36) | copy-start | bytes 4612
  8.2 71.2 %copy-start.8 = (bf16[768]{0:T(1024)(128)(2,1)S(1)}, bf16[768]{0:T(1024)(128)(2,1)}, u32[]{:S(2)}) copy-start(bf16[768]{0:T(1024)(128)(2,1)} %param.37) | copy-start | bytes 4612
  8.2 71.2 %copy-start.9 = (bf16[768]{0:T(1024)(128)(2,1)S(1)}, bf16[768]{0:T(1024)(128)(2,1)}, u32[]{:S(2)}) copy-start(bf16[768]{0:T(1024)(128)(2,1)} %param.38) | copy-start | bytes 4612

commit v2 on v1

--- a/solution.py
+++ b/solution.py
@@ -191,8 +191,8 @@
 
 def front_sync_kernel(
     p0, p1, p2, p3, k_hbm, vec, wq, wk, wv,
-    wd, pre_ref, xp, h0, h1, h2, h3, qkv, ot, lse_ref, rows_ref, w_own, m0, m1, m2, m3,
-    kg, load_s, wt, taps, zt, rf, slots, y_ref, t_ref, first, wz, vt, o1, o2, o3, frame_s, frame_r, gat_s, gat_r, mix_s, mix_r,
+    wd_out, pre_out, xp_out, h0_out, h1_out, h2_out, h3_out, qkv_out, ot, lse_ref, rows_ref, w_own, m0, m1, m2, m3,
+    wd, pre_ref, xp, h0, h1, h2, h3, qkv, store_s, kg, load_s, wt, taps, zt, rf, slots, y_ref, t_ref, first, wz, vt, o1, o2, o3, frame_s, frame_r, gat_s, gat_r, mix_s, mix_r,
 ):
     n, me = lax.axis_index("narrow"), lax.axis_index("wide")
     barrier = pltpu.get_barrier_semaphore()
@@ -212,6 +212,13 @@
             device_id_type=pl.DeviceIdType.MESH,
         )
 
+    stores = [
+        pltpu.make_async_copy(src, dst, store_s.at[i])
+        for i, (src, dst) in enumerate(
+            ((wd, wd_out), (pre_ref, pre_out), (xp, xp_out), (h0, h0_out), (h1, h1_out), (h2, h2_out), (h3, h3_out),
+             (qkv, qkv_out))
+        )
+    ]
     frames = [copy(r, (p1, p2, p3)[r - 1], rf.at[r - 1], frame_s.at[r - 1], frame_r.at[r - 1]) for r in (3, 1, 2)]
     for c in frames:
         c.start()
@@ -238,6 +245,7 @@
 
     for c in frames:
         c.wait()
+    stores[0].start()
     for c in range(2):
         xp[c, 0:64, :] = jnp.zeros((64, 128), bf16)
         xp[c, 1600:1664, :] = jnp.zeros((64, 128), bf16)
@@ -297,6 +305,8 @@
     for i in (1, 2):
         for r in (1, 2):
             direct(i, r).start()
+    for i in (1, 2, 3):
+        stores[i].start()
     for i in range(3):
         for r in (1, 2):
             direct(i, r).wait()
@@ -304,6 +314,8 @@
     for i in range(3):
         for r in (1, 2):
             relay(i, r).wait()
+    for i in (4, 5, 6):
+        stores[i].start()
 
     def project(row, rows, half):
         row0 = 64 * (1 - half)
@@ -317,6 +329,7 @@
         qkv[768 + 384 * half : 1152 + 384 * half, :] = project(384, 384, half)
         qkv[SLOTS + 96 * half : SLOTS + 96 * half + 96, :] = project(768, 96, half)
     qkv[SLOTS + SROWS : TROWS, :] = jnp.zeros((TROWS - SLOTS - SROWS, 768), bf16)
+    stores[7].start()
     vt[...] = qkv[:, 512:704].astype(f32).T.astype(bf16)
 
     outs = (m0, o1, o2, o3)
@@ -370,7 +383,7 @@
     rows_ref[0:FR, :] = own.astype(bf16)
     rows_ref[FR : FR + 96, :] = extra0.astype(bf16)
     rows_ref[FR + 96 : FR + 192, :] = extra1.astype(bf16)
-    for c in sent:
+    for c in sent + stores:
         c.wait()
 
 
@@ -381,13 +394,22 @@
     return pl.pallas_call(
         front_sync_kernel,
         in_specs=[vmem()] * 4 + [pl.BlockSpec(memory_space=pl.ANY)] + [vmem()] * 4,
-        out_specs=[vmem()] * 16,
+        out_specs=[pl.BlockSpec(memory_space=pl.ANY)] * 8 + [vmem()] * 8,
         out_shape=[sds((4, 512, 1024), bf16), sds((2, TROWS, 128), f32), sds((2, 1936, 128), bf16)]
         + [sds((864, 384), bf16)] * 4
         + [sds((TROWS, 768), bf16), sds((CH, TROWS), f32), sds((8, TROWS), f32), sds((576, 768), bf16)]
         + [sds((768, 768), bf16)]
         + [sds((CH, 640), bf16)] * 4,
         scratch_shapes=[
+            room(4, 512, 1024),
+            pltpu.VMEM((2, TROWS, 128), f32),
+            room(2, 1936, 128),
+            room(864, 384),
+            room(864, 384),
+            room(864, 384),
+            room(864, 384),
+            room(TROWS, 768),
+            sem((8,)),
             room(4, 48, 48, 128),
             sem,
             room(4, 512, 1024),
@@ -1053,67 +1075,80 @@
     )(gsum, pre, xp, sums, up_sum, wd, ffn_halves, qkv_halves)
 
 
-def unpack_frames_kernel(s_ref, c0, c1, c2, c3, o_ref):
-    me, li = s_ref[0], s_ref[1]
+def results_kernel(
+    s_ref, c0, c1, c2, c3, own1, other1, own2, other2, ownb, otherb, ownc, otherc,
+    frames, up, down, out, wq, wk, wv, small, gk_hbm, tiny,
+    gk, sems,
+):
+    me, li, core = s_ref[0], s_ref[1], s_ref[2]
+
+    def half(h, own, other):
+        return jnp.where(core == h, own, other)
+
+    stores = []
+    for g in range(16):
+        slot = g % 8
+        if g >= 8:
+            stores[g - 8].wait()
+        rel = me ^ (g // 4)
+        h, row = (g // 2) % 2, 96 * (g % 2)
+        x = half(h, ownc[rel, row : row + 96], otherc[rel, row : row + 96]).astype(f32)
+        for k2 in range(2):
+            for b in range(16):
+                gk[slot, 16 * k2 + b] = x[48 * k2 : 48 * k2 + 48, 48 * b : 48 * b + 48]
+        stores.append(pltpu.make_async_copy(gk.at[slot], gk_hbm.at[:, g], sems.at[g]))
+        stores[g].start()
+    for h in range(2):
+        tiny[h] = half(h, ownc[0, 192:208], otherc[0, 192:208])
+
     r_i, c_i = iota2((256, 768))
     top = jnp.zeros((256, 768), f32)
     low = jnp.zeros((256, 768), f32)
+    totals = [jnp.zeros((CH, 768), f32)] * 3
+    qkv = jnp.concatenate(
+        [jnp.concatenate([half(h, ownb[r], otherb[r]) for h in range(2)], axis=0) for r in range(4)], axis=0
+    )
     for r, chunk in enumerate((c0, c1, c2, c3)):
         base = 192 * (me ^ r)
         inside = (c_i >= base) & (c_i < base + 192)
-        top += mm(chunk[:, 0:256], ((c_i - base == r_i) & inside).astype(f32).astype(bf16))
-        low += mm(chunk[:, 128:384], ((c_i - base == r_i - 64) & inside).astype(f32).astype(bf16))
-    o_ref[li, 0:256, :] = top.astype(bf16)
-    o_ref[li, 256:384, :] = low[0:128].astype(bf16)
+        at0, at64 = (((c_i - base == r_i - skip) & inside).astype(f32).astype(bf16) for skip in (0, 64))
+        top += mm(chunk[:, 0:256], at0)
+        low += mm(chunk[:, 128:384], at64)
+        for k, (lane0, move) in enumerate(((0, at0), (128, at64), (384, at0))):
+            totals[k] = totals[k] + mm(qkv[192 * r : 192 * r + 192, lane0 : lane0 + 256], move)
+    wq[...], wk[...], wv[...] = totals
+    frames[li, 0:256, :] = top.astype(bf16)
+    frames[li, 256:384, :] = low[0:128].astype(bf16)
     slot = me * FR + lax.broadcasted_iota(jnp.int32, (128, 768), 0)
-    o_ref[1 - li, 0:128, :] = jnp.where(slot < SHORT, low[128:], 0.0).astype(bf16)
-    o_ref[1 - li, 128:384, :] = jnp.zeros((256, 768), bf16)
-
-
-def unpack_frames(scal, chunks):
+    frames[1 - li, 0:128, :] = jnp.where(slot < SHORT, low[128:], 0.0).astype(bf16)
+    frames[1 - li, 128:384, :] = jnp.zeros((256, 768), bf16)
+
+    for j in range(4):
+        at = slice(192 * (j % 2), 192 * (j % 2) + 192)
+        up[:, 768 * j : 768 * j + 768] = half(j // 2, own1[at, :], other1[at, :]).astype(f32)
+    down[0:496, :] = half(0, own2[...], other2[...]).astype(f32)
+    low_half = half(1, own2[...], other2[...]).astype(f32)
+    down[496:768, :] = low_half[0:272]
+    out[...] = low_half[272:464]
+    small[...] = low_half[464:480]
+    for store in stores[8:]:
+        store.wait()
+
+
+def results(scal, *parts):
+    sds = jax.ShapeDtypeStruct
     return pl.pallas_call(
-        unpack_frames_kernel,
-        in_specs=[smem()] + [vmem()] * 4,
-        out_specs=vmem(),
-        out_shape=jax.ShapeDtypeStruct((2, FR, 768), bf16),
+        results_kernel,
+        in_specs=[smem()] + [vmem()] * 12,
+        out_specs=[vmem()] * 8 + [pl.BlockSpec(memory_space=pl.ANY), vmem()],
+        out_shape=[sds((2, FR, 768), bf16), sds((CH, 3072), f32), sds((768, 768), f32)]
+        + [sds((CH, 768), f32)] * 4
+        + [sds((16, 768), f32), sds((32, 16, 48, 48), f32), sds((2, 16, 768), bf16)],
+        scratch_shapes=[pltpu.VMEM((8, 32, 48, 48), f32), pltpu.SemaphoreType.DMA((16,))],
         compiler_params=params(),
-        cost_estimate=cost(3),
-        name="unpack_frames",
-    )(scal, *chunks)
-
-
-def kernel_out_kernel(s_ref, own_ref, other_ref, o_ref, small_ref):
-    core = s_ref[2]
-    for g in range(4):
-        half, row = g >> 1, 96 * (g & 1)
-        x = jnp.where(half == core, own_ref[0, row : row + 96], other_ref[0, row : row + 96]).astype(f32)
-        for k2 in range(2):
-            for b in range(16):
-                o_ref[16 * k2 + b, g] = x[48 * k2 : 48 * k2 + 48, 48 * b : 48 * b + 48]
-
-    @pl.when(pl.program_id(0) == s_ref[0])
-    def _():
-        for half in range(2):
-            small_ref[half] = jnp.where(half == core, own_ref[0, 192:208], other_ref[0, 192:208])
-
-
-def kernel_out(scal, own, other):
-    return pl.pallas_call(
-        kernel_out_kernel,
-        grid_spec=pltpu.PrefetchScalarGridSpec(
-            num_scalar_prefetch=1,
-            grid=(4,),
-            in_specs=[pl.BlockSpec((1, 208, 768), lambda i, s: (i ^ s[0], 0, 0))] * 2,
-            out_specs=[
-                pl.BlockSpec((32, 4, 48, 48), lambda i, s: (0, i, 0, 0)),
-                pl.BlockSpec((2, 16, 768), lambda i, s: (0, 0, 0)),
-            ],
-        ),
-        out_shape=[jax.ShapeDtypeStruct((32, 16, 48, 48), f32), jax.ShapeDtypeStruct((2, 16, 768), bf16)],
-        compiler_params=params(),
-        cost_estimate=cost(9),
-        name="kernel_grad_out",
-    )(scal, own, other)
+        cost_estimate=cost(12),
+        name="results",
+    )(scal, *parts)
 
 
 def norm(v):
@@ -1258,49 +1293,6 @@
     return lax.dot_general(a, b, (((0,), (0,)), ((), ())), preferred_element_type=f32)
 
 
-def finish_kernel(s_ref, own1, other1, own2, other2, ownb, otherb, up, down, out, wq, wk, wv, small, a1, a2, b_ref):
-    me, core = s_ref[0], s_ref[2]
-    for buf, own, other in ((a1, own1, other1), (a2, own2, other2)):
-        buf[core] = own[...]
-        buf[1 - core] = other[...]
-    b_ref[:, pl.ds(pl.multiple_of(96 * core, 32), 96), :] = ownb[...]
-    b_ref[:, pl.ds(pl.multiple_of(96 - 96 * core, 32), 96), :] = otherb[...]
-    for j in range(4):
-        row = 192 * (j & 1)
-        up[:, 768 * j : 768 * j + 768] = a1[j >> 1, row : row + 192, :].astype(f32)
-    down[0:496, :] = a2[0].astype(f32)
-    down[496:768, :] = a2[1, 0:272, :].astype(f32)
-    out[...] = a2[1, 272:464, :].astype(f32)
-    small[...] = a2[1, 464:480, :].astype(f32)
-    r_i, c_i = iota2((256, 768))
-    totals = [jnp.zeros((CH, 768), f32)] * 3
-    for r in range(4):
-        base = 192 * (me ^ r)
-        inside = (c_i >= base) & (c_i < base + 192)
-        at0, at64 = (((c_i - base == r_i - skip) & inside).astype(f32).astype(bf16) for skip in (0, 64))
-        for k, (lane0, move) in enumerate(((0, at0), (128, at64), (384, at0))):
-            totals[k] = totals[k] + mm(b_ref[r, :, lane0 : lane0 + 256], move)
-    wq[...], wk[...], wv[...] = totals
-
-
-def finish(scal, *parts):
-    sds = jax.ShapeDtypeStruct
-    return pl.pallas_call(
-        finish_kernel,
-        in_specs=[smem()] + [vmem()] * 6,
-        out_specs=[vmem()] * 7,
-        out_shape=[sds((CH, 3072), f32), sds((768, 768), f32)] + [sds((CH, 768), f32)] * 4 + [sds((16, 768), f32)],
-        scratch_shapes=[
-            pltpu.VMEM((2, 384, 768), bf16),
-            pltpu.VMEM((2, 496, 768), bf16),
-            pltpu.VMEM((4, CH, 640), bf16),
-        ],
-        compiler_params=params(),
-        cost_estimate=cost(6),
-        name="weight_grads_out",
-    )(scal, *parts)
-
-
 def on_device(
     frames_in, lengths, kernel, conv_bias, w_query, b_query, w_key, w_value, b_value, w_out, b_out,
     gain_one, shift_one, w_up, b_up, w_down, b_down, gain_two, shift_two, out_grad,
@@ -1328,9 +1320,9 @@
     own1, own2, ownb, ownc, other1, other2, otherb, otherc, *fchunks = conv_sync(
         gsum, pre, xp, qkv_sums, up_sum, wd, ffn_halves, qkv_halves
     )
-    frames_grad = unpack_frames(scal, fchunks)
-    up, down, out, wq, wk, wv, small = finish(scal, own1, other1, own2, other2, ownb, otherb)
-    grad_kernel, tiny = kernel_out(scal, ownc, otherc)
+    frames_grad, up, down, out, wq, wk, wv, small, grad_kernel, tiny = results(
+        scal, *fchunks, own1, other1, own2, other2, ownb, otherb, ownc, otherc
+    )
     tiny = tiny.astype(f32)
 
     def mine(row):

time: 311 us -> 303 us (0.974)
  Pallas kernels: 294 us -> 286 us
    pallas_call x3 -> x1, Pallas kernels: 17 us -> 12.8 us  [results(): pl.pallas_call(results_kernel, in_specs=[smem()] + [vmem()] * 12, out_spe...]
    pallas_call x1, Pallas kernels: 70.5 us -> 66.8 us  [front_sync(): pl.pallas_call(front_sync_kernel, in_specs=[vmem()] * 4 + [pl.BlockSpec(m...]
where the time goes in v2:
time: 303 us; the launch traced here: 300 us
  Pallas kernels  286 us (94%)
  local copies, waits for them, and re-layouts  7.78 us (3%)
  other arithmetic  3.31 us (1%)
    pallas_call x1, Pallas kernels, conv_sync(): pl.pallas_call(conv_sync_kernel, in_specs=[vmem()] * 5 + [hbm] * 2 + [vme...  105 us
    pallas_call x1, Pallas kernels, attn_sync(): pl.pallas_call(attn_sync_kernel, in_specs=[hbm] * 2 + [vmem()] * 6 + [hbm...  69.1 us
    pallas_call x1, Pallas kernels, front_sync(): pl.pallas_call(front_sync_kernel, in_specs=[vmem()] * 4 + [pl.BlockSpec(m...  66.8 us
    pallas_call x1, Pallas kernels, ffn(): pl.pallas_call(ffn_kernel, in_specs=[smem()] + [vmem()] * 6 + [hbm, vmem(...  28.8 us
    pallas_call x1, Pallas kernels, results(): pl.pallas_call(results_kernel, in_specs=[smem()] + [vmem()] * 12, out_spe...  12.8 us

profile of v2, /device:TPU:0, one launch (start us, length us, event | category | flops | bytes accessed | tf_op | source)
XLA Modules:
  0.0 299.7 jit_solution(11977467684523493842)
XLA Ops:
  0.7 1.3 fusion.2
  3.3 0.6 pad_add_fusion.s_ref
  3.9 0.0 copy-start.1
  3.9 0.0 copy-start.2
  3.9 0.0 copy-start.3
  3.9 3.4 %pack_frames.1 = (bf16[256,384]{1,0:T(8,128)(2,1)}, bf16[256,384]{1,0:T(8,128)(2,1)}, bf16[256,384]{1,0:T(8,128)(2,1)}, bf16[256,384]{1,0:T(8,128)(2,1)}) custom-call(s32[4]{0:T(128)} %pad_add_fusion.s_ref, bf16[2,384,768]{2,1,0:T(8,128)(2,1)} %x_ref.1), custom_call_target="tpu_custom_call" | custom-call | flops 3000000000 | bytes 10200000 | tf_op jit(solution)/shard_map/pack_frames/pallas_call | solution.py:131
  7.3 0.0 copy-done.1
  7.3 0.0 copy-done.2
  7.3 0.0 copy-done.3
  7.4 0.1 pad.5.clone
  7.5 0.7 maximum_maximum_fusion.vec
  8.1 0.0 copy-start
  8.1 0.0 copy-start.4
  8.1 0.0 copy-start.5
  8.1 0.0 copy-start.6
  8.2 0.0 copy-start.7
  8.2 0.0 copy-start.8
  8.2 0.0 copy-start.9
  8.2 66.8 %front_sync.1 = (bf16[4,512,1024]{2,1,0:T(8,128)(2,1)}, f32[2,1792,128]{2,1,0:T(8,128)}, bf16[2,1936,128]{2,1,0:T(8,128)(2,1)}, bf16[864,384]{1,0:T(8,128)(2,1)}...) custom-call(bf16[256,384]{1,0:T(8,128)(2,1)} %get-tuple-element.78.p, ...), custom_call_target="tpu_custom_call" | custom-call | flops 65000001536 | bytes 221000000 | tf_op jit(solution)/shard_map/front_sync/pallas_call | solution.py:394
  75.0 0.0 copy-done
  75.0 0.6 broadcast_in_dim.11
  75.6 0.0 copy-done.4
  75.7 0.0 copy-done.5
  75.7 0.0 copy-done.6
  75.7 0.0 copy-done.7
  75.7 0.0 copy-done.8
  75.7 0.0 copy-done.9
  75.8 0.6 convert_element_type.7.vecs
  76.4 28.8 %ffn.1 = (bf16[2,384,768]{2,1,0:T(8,128)(2,1)}, bf16[768,3072]{1,0:T(8,128)(2,1)}, bf16[768,3072]{1,0:T(8,128)(2,1)}, bf16[768,768]{1,0:T(8,128)(2,1)}, bf16[768...) custom-call(s32[4]{0:T(128)} %pad_add_fusion.s_ref, ...), custom_call_target="tpu_custom_call" | custom-call | flops 28000000000 | bytes 95200000 | tf_op jit(solution)/shard_map/ffn/pallas_call | solution.py:1265
  105.2 69.1 %attn_sync.1 = (bf16[384,768]{1,0:T(8,128)(2,1)}, bf16[4,496,768]{2,1,0:T(8,128)(2,1)}, bf16[4,96,640]{2,1,0:T(8,128)(2,1)}, f32[192,1792]{1,0:T(8,128)}, f32[1,768]{1,0:T(1,128)}) custom-call(bf16[1792,768]{1,0:T(8,128)(2,1)} %get-tuple-element.88.qkv_hbm, f32[192,1792]{1,0:T(8,128)} %get-tuple-element.89.ot_hbm, f32[8,1792]{1,0:T(8,128)} %get-tuple-element.90.lse_ref, ...), custom_call_target="tpu_custom_call" | custom-call | flops 89999998976 | bytes 306000000 | tf_op jit(solution)/shard_map/attn_sync/pallas_call | solution.py:783
  174.3 105.0 %conv_sync.1 = (bf16[384,768]{1,0:T(8,128)(2,1)}, bf16[496,768]{1,0:T(8,128)(2,1)}, bf16[4,96,640]{2,1,0:T(8,128)(2,1)}, bf16[4,208,768]{2,1,0:T(8,128)(2,1)}, b...) custom-call(f32[192,1792]{1,0:T(8,128)} %get-tuple-element.107.gsum,, ...), custom_call_target="tpu_custom_call" | custom-call | flops 99999997952 | bytes 340000000 | tf_op jit(solution)/shard_map/conv_sync/pallas_call | solution.py:1047
  279.3 12.8 %results.1 = (bf16[2,384,768]{2,1,0:T(8,128)(2,1)}, f32[192,3072]{1,0:T(8,128)}, f32[768,768]{1,0:T(8,128)}, f32[192,768]{1,0:T(8,128)}, f32[192,768]{1,0:T(8,12...) custom-call(s32[4]{0:T(128)} %pad_add_fusion.s_ref, ...), custom_call_target="tpu_custom_call" | custom-call | flops 12000000000 | bytes 40800000 | tf_op jit(solution)/shard_map/results/pallas_call | solution.py:1140
  292.1 0.8 convert_element_type.8
  292.9 0.1 concatenate.13
  293.0 0.1 concatenate.12
  293.1 0.6 reshape.57
  293.8 1.2 fusion.1
  295.0 0.9 fusion
  295.9 0.6 constant_dynamic-slice_fusion.4
  296.6 0.6 constant_dynamic-slice_fusion.2
  297.2 0.7 slice.52
  297.9 0.6 dynamic-slice_reduce_fusion
  298.5 0.6 constant_dynamic-slice_fusion
  (13 shorter events, 0.1 us)
Async XLA Ops:
  3.9 3.4 %copy-start.1 = (bf16[768]{0:T(1024)(128)(2,1)S(1)}, bf16[768]{0:T(1024)(128)(2,1)}, u32[]{:S(2)}) copy-start(bf16[768]{0:T(1024)(128)(2,1)} %param.28) | copy-start | bytes 4612
  3.9 3.4 %copy-start.2 = (bf16[768]{0:T(1024)(128)(2,1)S(1)}, bf16[768]{0:T(1024)(128)(2,1)}, u32[]{:S(2)}) copy-start(bf16[768]{0:T(1024)(128)(2,1)} %param.25) | copy-start | bytes 4612
  3.9 3.5 %copy-start.3 = (bf16[768]{0:T(1024)(128)(2,1)S(1)}, bf16[768]{0:T(1024)(128)(2,1)}, u32[]{:S(2)}) copy-start(bf16[768]{0:T(1024)(128)(2,1)} %param.23) | copy-start | bytes 4612
  8.1 66.9 %copy-start = (bf16[3072]{0:T(1024)(128)(2,1)S(1)}, bf16[3072]{0:T(1024)(128)(2,1)}, u32[]{:S(2)}) copy-start(bf16[3072]{0:T(1024)(128)(2,1)} %param.34) | copy-start | bytes 18436
  8.1 67.5 %copy-start.4 = (bf16[768]{0:T(1024)(128)(2,1)S(1)}, bf16[768]{0:T(1024)(128)(2,1)}, u32[]{:S(2)}) copy-start(bf16[768]{0:T(1024)(128)(2,1)} %param.30) | copy-start | bytes 4612
  8.1 67.5 %copy-start.5 = (bf16[768]{0:T(1024)(128)(2,1)S(1)}, bf16[768]{0:T(1024)(128)(2,1)}, u32[]{:S(2)}) copy-start(bf16[768]{0:T(1024)(128)(2,1)} %param.31) | copy-start | bytes 4612
  8.1 67.5 %copy-start.6 = (bf16[768]{0:T(1024)(128)(2,1)S(1)}, bf16[768]{0:T(1024)(128)(2,1)}, u32[]{:S(2)}) copy-start(bf16[768]{0:T(1024)(128)(2,1)} %param.32) | copy-start | bytes 4612
  8.2 67.5 %copy-start.7 = (bf16[768]{0:T(1024)(128)(2,1)S(1)}, bf16[768]{0:T(1024)(128)(2,1)}, u32[]{:S(2)}) copy-start(bf16[768]{0:T(1024)(128)(2,1)} %param.36) | copy-start | bytes 4612
  8.2 67.6 %copy-start.8 = (bf16[768]{0:T(1024)(128)(2,1)S(1)}, bf16[768]{0:T(1024)(128)(2,1)}, u32[]{:S(2)}) copy-start(bf16[768]{0:T(1024)(128)(2,1)} %param.37) | copy-start | bytes 4612
  8.2 67.6 %copy-start.9 = (bf16[768]{0:T(1024)(128)(2,1)S(1)}, bf16[768]{0:T(1024)(128)(2,1)}, u32[]{:S(2)}) copy-start(bf16[768]{0:T(1024)(128)(2,1)} %param.38) | copy-start | bytes 4612
